TPU v7x, 128 devices: a whole 4x4x4 slice. The times are simulated.
128 devices in a mesh: seq: 64 (over y, z, x), dp: 2 (over core).
Axes of the slice: x: 4, y: 4, z: 4, core: 2. Of those that a mesh axis runs over, the one named last changes fastest.
Arguments:
- activation: bfloat16 [65536, 2048], P(('dp', 'seq')), parts along dimension 0, may hold values from -0.75 to 0.75
- step_size: float32 [65536, 32], P(('dp', 'seq')), parts along dimension 0, may hold values from 0 to 6, as said below
- decay_scale: float32 [64], P('dp'), parts along dimension 0, may hold values from -1 to 0
- write_vectors: bfloat16 [65536, 128], P(('dp', 'seq')), parts along dimension 0, may hold values from -3 to 3
- read_vectors: bfloat16 [65536, 128], P(('dp', 'seq')), parts along dimension 0, may hold values from -3 to 3
- upstream: bfloat16 [65536, 2048], P(('dp', 'seq')), parts along dimension 0, may hold values from -0.625 to 0.625
Outputs:
- activation_grad: bfloat16 [65536, 2048], P(('dp', 'seq')), parts along dimension 0
- logstep_grad: float32 [65536, 32], P(('dp', 'seq')), parts along dimension 0
- write_grad: float32 [65536, 128], P(('dp', 'seq')), parts along dimension 0
- readout_gradient: float32 [65536, 128], P(('dp', 'seq')), parts along dimension 0
There are 2 independent parts, one for each index of `dp`. A program takes and returns all parts, laid end to end along the dimension named above; each array names one. Nothing has to cross between parts.
Inputs may be any that keep to these rules, and one draw needn't show every extreme that they name: `step_size`: step sizes are positive.
All inputs are finite; a program needn't handle non-finite values.
Results may differ from a plain program's by a relative error of at most 0.0055.
Values sent between devices are 32-bit elements; how exact they have to be, the bound alone decides.
No kernel may reach another device: no remote copies, remote signals or barrier semaphores. Data moves between devices by JAX's collectives and lax.ppermute only.
A program may use at most 384 MiB of HBM per device.

v0:
```python
from functools import partial

import jax
import jax.numpy as jnp
from jax import lax
from jax.sharding import PartitionSpec as P

GROUP = 256


def carried_in(value, axis, join, neutral, backward):
    count, mine = (lax.axis_size(axis), lax.axis_index(axis))
    pieces = jax.tree.map(lambda part: lax.all_gather(part, axis), value)
    if backward:
        pieces = jax.tree.map(lambda part: part[::-1], pieces)
        mine = count - 1 - mine
    so_far = jax.tree.map(
        lambda part, zero: jnp.full_like(part, 0) + jnp.asarray(zero, part.dtype), value, neutral
    )

    def lap(position, so_far):
        longer = join(so_far, jax.tree.map(lambda part: part[position], pieces))
        return jax.tree.map(lambda new, old: jnp.where(position < mine, new, old), longer, so_far)

    return lax.fori_loop(0, count - 1, lap, so_far)


def join_carry(earlier, later):
    return (earlier[0] * later[0], later[0][:, None, None] * earlier[1] + later[1])


def lower_table(row_count):
    return (
        lax.broadcasted_iota(jnp.int32, (row_count, row_count), 0)
        >= lax.broadcasted_iota(jnp.int32, (row_count, row_count), 1)
    ).astype(jnp.float32)


def group_local(blocks, decay_scale):
    activation, upstream, write_vectors, read_vectors, step_size = blocks
    row_count = activation.shape[0]
    head_count = decay_scale.shape[0]
    head_width = activation.shape[1] // head_count
    act_three = activation.reshape(row_count, head_count, head_width)
    up_three = upstream.reshape(row_count, head_count, head_width)
    log_decay = step_size * decay_scale[None, :]
    cumulative = jnp.dot(
        lower_table(row_count),
        log_decay,
        precision=lax.Precision.HIGHEST,
        preferred_element_type=jnp.float32,
    )
    total_log = cumulative[-1]
    later_mask = lax.broadcasted_iota(jnp.int32, (row_count, row_count), 0) >= lax.broadcasted_iota(
        jnp.int32, (row_count, row_count), 1
    )
    gap_log = cumulative.T[:, :, None] - cumulative.T[:, None, :]
    decay_pairs = jnp.where(
        later_mask[None], jnp.exp(jnp.where(later_mask[None], gap_log, 0.0)), 0.0
    )
    pair_dots = jnp.einsum("thp,shp->hts", up_three, act_three, preferred_element_type=jnp.float32)
    scores = jnp.dot(read_vectors, write_vectors.T, preferred_element_type=jnp.float32)
    weighted = decay_pairs * pair_dots * step_size.T[:, None, :]
    coupled = scores[None] * weighted
    net_rows = jnp.sum(coupled, axis=2).T - jnp.sum(coupled, axis=1).T
    pair_sum = jnp.sum(weighted, axis=0).astype(jnp.bfloat16)
    write_part = jnp.einsum("ts,tn->sn", pair_sum, read_vectors, preferred_element_type=jnp.float32)
    read_part = jnp.dot(pair_sum, write_vectors, preferred_element_type=jnp.float32)
    masked = (decay_pairs * scores[None]).astype(jnp.bfloat16)
    back_local = jnp.einsum("hts,thp->shp", masked, up_three, preferred_element_type=jnp.float32)
    decay_in = jnp.exp(cumulative)
    decay_out = jnp.exp(total_log[None, :] - cumulative)
    act_scaled = (act_three * (step_size * decay_out)[:, :, None]).astype(jnp.bfloat16)
    up_scaled = (up_three * decay_in[:, :, None]).astype(jnp.bfloat16)
    state_part = jnp.einsum(
        "sn,shp->hnp", write_vectors, act_scaled, preferred_element_type=jnp.float32
    )
    grad_part = jnp.einsum(
        "un,uhp->hnp", read_vectors, up_scaled, preferred_element_type=jnp.float32
    )
    return (
        log_decay,
        decay_in,
        decay_out,
        net_rows,
        write_part,
        read_part,
        back_local,
        act_scaled,
        up_scaled,
        state_part,
        grad_part,
        jnp.exp(total_log),
    )


def on_device(activation, step_size, decay_scale, write_vectors, read_vectors, upstream):
    row_count, inner_width = activation.shape
    head_count = decay_scale.shape[0]
    head_width = inner_width // head_count
    state_width = write_vectors.shape[1]
    block_count = row_count // GROUP
    blocks = (
        activation.reshape(block_count, GROUP, inner_width),
        upstream.reshape(block_count, GROUP, inner_width),
        write_vectors.reshape(block_count, GROUP, state_width),
        read_vectors.reshape(block_count, GROUP, state_width),
        step_size.reshape(block_count, GROUP, head_count),
    )
    (
        log_decay,
        decay_in,
        decay_out,
        net_rows,
        write_part,
        read_part,
        back_local,
        act_scaled,
        up_scaled,
        state_part,
        grad_part,
        block_decay,
    ) = lax.map(partial(group_local, decay_scale=decay_scale), blocks)
    single_decay_factor = jnp.ones((head_count,), jnp.float32)
    zero_state = jnp.zeros((head_count, state_width, head_width), jnp.float32)
    device_decay, device_state = (single_decay_factor, zero_state)
    for block_index in range(block_count):
        device_decay, device_state = join_carry(
            (device_decay, device_state), (block_decay[block_index], state_part[block_index])
        )
    device_grad = zero_state
    for block_index in reversed(range(block_count)):
        device_grad = join_carry(
            (single_decay_factor, device_grad), (block_decay[block_index], grad_part[block_index])
        )[1]
    enter_pair = carried_in(
        (device_decay, device_state), "seq", join_carry, (single_decay_factor, zero_state), False
    )
    leave_pair = carried_in(
        (device_decay, device_grad), "seq", join_carry, (single_decay_factor, zero_state), True
    )
    enter_device = enter_pair[1]
    leave_device = leave_pair[1]
    enter_list = []
    end_list = []
    running_state = enter_device
    for block_index in range(block_count):
        enter_list.append(running_state)
        running_state = (
            block_decay[block_index][:, None, None] * running_state + state_part[block_index]
        )
        end_list.append(running_state)
    leave_list = [None] * block_count
    running_grad = leave_device
    for block_index in reversed(range(block_count)):
        leave_list[block_index] = running_grad
        running_grad = (
            grad_part[block_index] + block_decay[block_index][:, None, None] * running_grad
        )
    enter_state = jnp.stack(enter_list)
    leave_end = jnp.stack(end_list)
    leave_grad = jnp.stack(leave_list)
    enter_low = enter_state.astype(jnp.bfloat16)
    leave_low = leave_grad.astype(jnp.bfloat16)
    act_four = blocks[0].reshape(block_count, GROUP, head_count, head_width)
    up_four = blocks[1].reshape(block_count, GROUP, head_count, head_width)
    three_step_count = blocks[4]
    offset = jnp.einsum("ctn,chnp->cthp", blocks[3], enter_low, preferred_element_type=jnp.float32)
    row_cross = decay_in * jnp.sum(offset * up_four, axis=3)
    read_cross = jnp.einsum(
        "cthp,chnp->ctn", up_scaled, enter_low, preferred_element_type=jnp.float32
    )
    back_cross = jnp.einsum(
        "csn,chnp->cshp", blocks[2], leave_low, preferred_element_type=jnp.float32
    )
    back_total = back_local + decay_out[:, :, :, None] * back_cross
    write_cross = jnp.einsum(
        "cshp,chnp->csn", act_scaled, leave_low, preferred_element_type=jnp.float32
    )
    col_cross = three_step_count * decay_out * jnp.sum(act_four * back_cross, axis=3)
    net = net_rows + row_cross - col_cross
    boundary = jnp.sum(leave_grad * leave_end, axis=(2, 3))
    upper_table = lower_table(GROUP).T
    suffix_sums = jnp.einsum(
        "ts,csh->cth",
        upper_table,
        net,
        precision=lax.Precision.HIGHEST,
        preferred_element_type=jnp.float32,
    )
    logarithm_gradient = suffix_sums + boundary[:, None, :]
    activation_grad = (
        (three_step_count[:, :, :, None] * back_total)
        .astype(jnp.bfloat16)
        .reshape(row_count, inner_width)
    )
    logstep_grad = (
        three_step_count * jnp.sum(act_four * back_total, axis=3) + log_decay * logarithm_gradient
    ).reshape(row_count, head_count)
    write_grad = (write_part + write_cross).reshape(row_count, state_width)
    readout_gradient = (read_part + read_cross).reshape(row_count, state_width)
    return (activation_grad, logstep_grad, write_grad, readout_gradient)


def solution(mesh):
    return jax.shard_map(
        on_device,
        mesh=mesh,
        in_specs=(
            P(("dp", "seq"), None),
            P(("dp", "seq"), None),
            P("dp"),
            P(("dp", "seq"), None),
            P(("dp", "seq"), None),
            P(("dp", "seq"), None),
        ),
        out_specs=(
            P(("dp", "seq"), None),
            P(("dp", "seq"), None),
            P(("dp", "seq"), None),
            P(("dp", "seq"), None),
        ),
        check_vma=False,
    )
```

profile of v0, /device:TPU:0, one launch (start us, length us, event | category | flops | bytes accessed | tf_op | source)
XLA Modules:
  0.0 1078.9 jit_solution(702497192728637028)
XLA Ops:
  8.8 42.7 %while.60 = (s32[]{:T(128)}, f32[2,256,32]{1,2,0:T(8,128)}, f32[2,256,32]{1,2,0:T(8,128)}, f32[2,256,32]{1,2,0:T(8,128)}, f32[2,256,32]{1,2,0:T(8,128)}, /*index...) while((s32[]{:T(128)}, f32[2,256,32]{1,2,0:T(8,128)}, ...), condition=%wide.region_4.5_spmd, body=%wide.region_0.4_spmd.sunk | while | flops 916553728 | bytes 120301168 | solution.py:123
  24.2 4.6 multiply_reduce_fusion.5
  45.6 4.6 multiply_reduce_fusion.5
  57.5 5.6 reshape.138
  63.0 7.5 reshape.139
  70.5 177.6 %all-gather = f32[64,1,32]{2,1,0:T(1,128)S(1)} all-gather(f32[1,1,32]{2,1,0:T(1,128)S(1)} %bitcast.279), channel_id=1, replica_groups=mesh['seq'=64,'dp'=2] {'seq'}, dimensions={0}, use_global_device_ids=true | all-gather | bytes 8320 | tf_op jit(solution)/shard_map/all_gather | solution.py:13
  248.2 7.9 copy.56
  256.1 8.0 copy.50
  264.1 69.8 %all-gather.6.cloned.1.call-done = f32[64,32,128,64]{2,3,1,0:T(8,128)} async-done(((f32[1,32,128,64]{2,3,1,0:T(8,128)}), f32[64,32,128,64]{2,3,1,0:T(8,128)}) %all-gather.6.cloned.1.call-update) | async-done | bytes 67108880 | tf_op jit(solution)/shard_map/all_gather | solution.py:13
  333.8 328.3 %while.62 = (s32[]{:T(128)}, f32[32,128,64]{2,1,0:T(8,128)}, s32[]{:T(128)}, f32[64,32]{1,0:T(8,128)S(1)}, f32[64,32,128,64]{2,3,1,0:T(8,128)}, /*index=5*/s32[]{:T(128)}, s32[]{:T(128)}) while((s32[]{:T(128)}, f32[32,128,64]{2,1,0:T(8,128)}, s32[]{:T(128)}, f32[64,32]{1,0:T(8,128)S(1)}, f32[64,32,128,64]{2,3,1,0:T(8,128)}, ...), condition=%wide.region_9.10_spmd.clone, body=%wide.region_8.9_spmd.clone.sunk | while | flops 1048580 | bytes 7340521 | solution.py:25
  370.6 3.3 fusion.130
  381.0 3.4 fusion.130
  391.5 3.4 fusion.130
  407.3 3.3 fusion.130
  428.1 3.9 fusion.130
  434.3 3.8 fusion.130
  450.5 3.4 fusion.130
  466.2 3.4 fusion.130
  482.0 3.4 fusion.130
  497.7 3.4 fusion.130
  508.2 3.4 fusion.130
  513.5 3.4 fusion.130
  524.0 3.4 fusion.130
  529.3 3.4 fusion.130
  539.9 3.4 fusion.130
  555.6 3.4 fusion.130
  666.5 43.7 %rev.7 = f32[64,32,128,64]{2,3,1,0:T(8,128)} reverse(f32[64,32,128,64]{2,3,1,0:T(8,128)} %all-gather.4.cloned.1.call-done), dimensions={0} | reverse | bytes 134217728 | tf_op jit(solution)/shard_map/rev | solution.py:15
  710.2 329.1 %while.61 = (s32[]{:T(128)}, f32[32,128,64]{2,1,0:T(8,128)}, s32[]{:T(128)}, f32[64,32]{1,0:T(8,128)S(1)}, f32[64,32,128,64]{2,3,1,0:T(8,128)}, /*index=5*/s32[]{:T(128)}, s32[]{:T(128)}) while((s32[]{:T(128)}, f32[32,128,64]{2,1,0:T(8,128)}, s32[]{:T(128)}, f32[64,32]{1,0:T(8,128)S(1)}, f32[64,32,128,64]{2,3,1,0:T(8,128)}, ...), condition=%wide.region_6.7_spmd.clone, body=%wide.region_5.6_spmd.clone.sunk | while | flops 1048580 | bytes 7340521 | solution.py:25
  715.8 3.3 fusion.129
  721.0 3.3 fusion.129
  731.5 3.3 fusion.129
  736.8 3.3 fusion.129
  747.3 3.3 fusion.129
  752.5 3.3 fusion.129
  763.0 3.3 fusion.129
  768.3 3.3 fusion.129
  784.0 3.3 fusion.129
  799.8 3.3 fusion.129
  805.0 3.3 fusion.129
  815.5 3.3 fusion.129
  820.8 3.3 fusion.129
  831.2 3.3 fusion.129
  836.5 3.3 fusion.129
  847.0 3.3 fusion.129
  852.2 3.3 fusion.129
  862.7 3.3 fusion.129
  868.0 3.3 fusion.129
  883.7 3.3 fusion.129
  899.5 3.3 fusion.129
  904.7 3.3 fusion.129
  915.2 3.3 fusion.129
  920.5 3.3 fusion.129
  931.0 3.3 fusion.129
  936.2 3.3 fusion.129
  946.7 3.3 fusion.129
  952.0 3.3 fusion.129
  962.5 3.3 fusion.129
  967.7 3.3 fusion.129
  983.5 3.3 fusion.129
  999.2 3.3 fusion.129
  1004.5 3.3 fusion.129
  1047.9 4.4 multiply_reduce_fusion.2
  1053.1 7.4 copy.65
  1060.5 6.8 reshape.137
  (657 shorter events, 548.6 us)
Async XLA Ops:
  7.2 326.7 %all-gather.6.cloned.1.call-start = ((), (), s32[]{:S(2)}) async-start(), calls=%async_computation.1 | async-start | bytes 68157440 | tf_op jit(solution)/shard_map/all_gather | solution.py:13
  14.5 0.9 copy-start.3
  14.5 1.7 copy-start.7
  14.5 2.3 copy-start.10
  15.0 1.9 copy-start.5
  16.2 2.2 copy-start.16
  16.6 3.4 copy-start.8
  17.3 2.8 copy-start.11
  18.4 2.6 copy-start.12
  20.1 3.2 copy-start.17
  21.0 2.3 copy-start.28
  21.0 2.4 copy-start.37
  23.3 5.5 copy-start.13
  24.2 4.6 copy-start.29
  24.2 4.6 copy-start.24
  24.2 4.9 copy-start.38
  24.2 5.1 copy-start.21
  24.2 5.1 copy-start.31
  24.2 5.1 copy-start.34
  29.1 1.0 copy-start.25
  29.3 0.7 copy-start.39
  29.4 0.7 copy-start.22
  35.8 0.9 copy-start.3
  35.8 1.7 copy-start.7
  35.8 2.3 copy-start.10
  36.3 1.9 copy-start.5
  37.5 2.2 copy-start.16
  37.9 3.3 copy-start.8
  38.6 2.7 copy-start.11
  39.7 2.6 copy-start.12
  41.3 3.3 copy-start.17
  42.3 2.3 copy-start.28
  42.3 2.4 copy-start.37
  44.6 5.5 copy-start.13
  45.5 4.6 copy-start.29
  45.5 4.6 copy-start.24
  45.5 4.9 copy-start.38
  45.5 5.1 copy-start.21
  45.5 5.1 copy-start.31
  45.5 5.1 copy-start.34
  50.4 1.1 copy-start.25
  50.6 0.7 copy-start.39
  50.7 0.7 copy-start.22
  50.7 0.7 copy-start.32
  50.8 0.7 copy-start.35
  54.5 612.0 %all-gather.4.cloned.1.call-start = ((), (), s32[]{:S(2)}) async-start(), calls=%async_computation | async-start | bytes 68157440 | tf_op jit(solution)/shard_map/all_gather | solution.py:13
  54.5 2.9 copy-start
  662.2 2.3 copy-start.9
  1039.3 4.5 copy-start.6
  1041.5 1.6 copy-start.14
  1041.5 1.8 copy-start.15
  1041.5 2.2 copy-start.19
  1041.5 2.2 copy-start.20
  1043.4 2.3 copy-start.2
  1045.6 2.2 copy-start.1
  1045.6 2.2 copy-start.4
  1045.6 2.2 copy-start.23
  1047.8 4.4 copy-start.27
  1047.8 4.4 copy-start.30
  1047.8 4.4 copy-start.33
  1047.8 4.4 copy-start.36
  1060.5 6.8 copy-start.40
  1067.3 3.2 copy-start.18
  1067.3 3.2 copy-start.26
  (2 other events, 1.3 us)
Sparse Core Ops, SparseCore 0:
  54.6 279.2 all-gather.5
  336.7 276.0 all-gather.3
where the time goes:
time: 1090 us; the launch traced here: 1080 us
  other arithmetic  429 us (39%)
  local copies, waits for them, and re-layouts  355 us (33%)
  blocking collectives  178 us (16%)
  waiting for transfers between devices  69.8 us (6%)
  matrix products  28.8 us (3%)
  between operations  14.4 us (1%)
    select_n x126, other arithmetic, lap(): jnp.where(position < mine, new, old)  412 us
    dynamic_slice x252, local copies, waits for them, and re-layouts, lap(): longer = join(so_far, jax.tree.map(lambda part: part[position], pieces))  241 us
    all_gather x1, blocking collectives, carried_in(): pieces = jax.tree.map(lambda part: lax.all_gather(part, axis), value)  178 us
    all_gather x2, waiting for transfers between devices, carried_in(): pieces = jax.tree.map(lambda part: lax.all_gather(part, axis), value)  69.8 us
    rev x2, local copies, waits for them, and re-layouts, carried_in(): pieces = jax.tree.map(lambda part: part[::-1], pieces)  43.7 us
  transfers between devices with their start and end apart: 2, of which 1 were waited for; matrix products, arithmetic and copies ran while one was open for 34% of the time, Pallas kernels for 0%

commit v1 on v0

v1 whole, which is shorter than its diff:
```python
import math
from functools import partial

import jax
import jax.numpy as jnp
from jax import lax
from jax.experimental import pallas as pl
from jax.experimental.pallas import tpu as pltpu
from jax.sharding import PartitionSpec as P

GROUP = 256
LANES = 128
BUNCH = 8
LOG2E = math.log2(math.e)
F32 = jnp.float32
BF16 = jnp.bfloat16
MIB = 1 << 20


def dot_nn(a, b):
    return jnp.dot(a, b, preferred_element_type=F32)


def dot_nt(a, b):
    return lax.dot_general(a, b, (((1,), (1,)), ((), ())), preferred_element_type=F32)


def dot_tn(a, b):
    return lax.dot_general(a, b, (((0,), (0,)), ((), ())), preferred_element_type=F32)


def exact_dot(table, value):
    high = value.astype(BF16)
    rest = value - high.astype(F32)
    middle = rest.astype(BF16)
    low = (rest - middle.astype(F32)).astype(BF16)
    return dot_nn(table, high) + dot_nn(table, middle) + dot_nn(table, low)


def left_half(rows):
    return lax.broadcasted_iota(jnp.int32, (rows, LANES), 1) < LANES // 2


def pair_lanes(columns, pair):
    return jnp.where(
        left_half(columns.shape[0]),
        columns[:, 2 * pair : 2 * pair + 1],
        columns[:, 2 * pair + 1 : 2 * pair + 2],
    )


def order_table(size, upper):
    row = lax.broadcasted_iota(jnp.int32, (size, size), 0)
    column = lax.broadcasted_iota(jnp.int32, (size, size), 1)
    return jnp.where(row <= column if upper else row >= column, 1.0, 0.0)


def states_kernel(
    heads, piece_rows, dt_ref, scale_ref, write_ref, read_ref, act_ref, up_ref,
    pieces_ref, early_ref, late_ref, shifted_ref, out_ref, in_ref, across_ref, spread_ref,
    act_buf, up_buf, piece_buf, early_buf, late_buf, in_sems, out_sems,
):
    rows = dt_ref.shape[0]
    blocks = rows // GROUP
    bunches = heads // BUNCH
    wide = BUNCH // 2 * LANES
    loads = []
    for bunch in range(bunches):
        for which, (source, target) in enumerate(((act_ref, act_buf), (up_ref, up_buf))):
            lanes = pl.ds(bunch * wide, wide)
            copy = pltpu.make_async_copy(
                source.at[:, lanes], target.at[:, lanes], in_sems.at[bunch, which]
            )
            copy.start()
            loads.append(copy)
    table = order_table(GROUP, False).astype(BF16)
    decay_in, decay_out, totals = [], [], []
    for block in range(blocks):
        span = slice(block * GROUP, (block + 1) * GROUP)
        dt = dt_ref[span, :]
        running = exact_dot(table, dt * scale_ref[...])
        total = running[GROUP - 1 : GROUP, :]
        entering = jnp.exp(running)
        leaving = dt * jnp.exp(total - running)
        shifted = running * LOG2E - jnp.log2(dt)
        padded = jnp.concatenate(
            [running * LOG2E, jnp.zeros((GROUP, LANES - heads), F32)], axis=1
        )
        across = padded.T
        for bunch in range(bunches):
            few = slice(bunch * BUNCH, (bunch + 1) * BUNCH)
            shifted_ref[bunch, span, :] = shifted[:, few]
            out_ref[bunch, span, :] = leaving[:, few]
            in_ref[bunch, span, :] = entering[:, few]
            across_ref[bunch, :, span] = across[few, :]
        decay_in.append(entering)
        decay_out.append(leaving)
        totals.append(total)
    block_decay = [jnp.exp(total) for total in totals]
    device_decay = jnp.exp(totals[0] + totals[1])
    write_across = [write_ref[b * GROUP : (b + 1) * GROUP, :].T for b in range(blocks)]
    read_across = [read_ref[b * GROUP : (b + 1) * GROUP, :].T for b in range(blocks)]
    per_pair = LANES // piece_rows
    stores = []
    for bunch in range(bunches):
        lanes = slice(bunch * wide, (bunch + 1) * wide)
        loads[2 * bunch].wait()
        loads[2 * bunch + 1].wait()
        state, grad = [], []
        for block in range(blocks):
            span = slice(block * GROUP, (block + 1) * GROUP)
            act_scaled, up_scaled = [], []
            for pair in range(bunch * BUNCH // 2, (bunch + 1) * BUNCH // 2):
                here = slice(pair * LANES, (pair + 1) * LANES)
                act_scaled.append(
                    (act_buf[span, here].astype(F32) * pair_lanes(decay_out[block], pair)).astype(BF16)
                )
                up_scaled.append(
                    (up_buf[span, here].astype(F32) * pair_lanes(decay_in[block], pair)).astype(BF16)
                )
            state.append(dot_nn(write_across[block], jnp.concatenate(act_scaled, axis=1)))
            grad.append(dot_nn(read_across[block], jnp.concatenate(up_scaled, axis=1)))
        first, second, both = (
            jnp.concatenate(
                [pair_lanes(decay, pair) for pair in range(bunch * BUNCH // 2, (bunch + 1) * BUNCH // 2)],
                axis=1,
            )
            for decay in (block_decay[0], block_decay[1], device_decay)
        )
        spread_ref[:, lanes] = jnp.concatenate([first, second, both, jnp.zeros((5, wide), F32)], axis=0)
        device_state = second * state[0] + state[1]
        device_grad = grad[0] + first * grad[1]
        early_buf[:, lanes] = state[0]
        late_buf[:, lanes] = grad[1]
        for local in range(BUNCH // 2):
            pair = bunch * BUNCH // 2 + local
            here = slice(local * LANES, (local + 1) * LANES)
            few = slice(pair * per_pair, (pair + 1) * per_pair)
            piece_buf[few, :piece_rows, :] = device_state[:, here].reshape(per_pair, piece_rows, LANES)
            piece_buf[few, piece_rows : 2 * piece_rows, :] = device_grad[:, here].reshape(
                per_pair, piece_rows, LANES
            )
            piece_buf[few, 2 * piece_rows :, :] = jnp.broadcast_to(
                both[:, here][None], (per_pair, 8, LANES)
            )
        few = pl.ds(bunch * BUNCH // 2 * per_pair, BUNCH // 2 * per_pair)
        copies = (
            (piece_buf.at[few], pieces_ref.at[few]),
            (early_buf.at[:, pl.ds(bunch * wide, wide)], early_ref.at[:, pl.ds(bunch * wide, wide)]),
            (late_buf.at[:, pl.ds(bunch * wide, wide)], late_ref.at[:, pl.ds(bunch * wide, wide)]),
        )
        for which, (source, target) in enumerate(copies):
            copy = pltpu.make_async_copy(source, target, out_sems.at[bunch, which])
            copy.start()
            stores.append(copy)
    for copy in stores:
        copy.wait()


def scan_kernel(piece_rows, got_ref, carried_ref):
    count = got_ref.shape[0]
    zero = jnp.zeros((piece_rows, LANES), F32)

    def lap(step, carry):
        state, grad = carry
        carried_ref[step, :piece_rows, :] = state
        state = got_ref[step, 2 * piece_rows : 2 * piece_rows + 1, :] * state + got_ref[step, :piece_rows, :]
        back = count - 1 - step
        carried_ref[back, piece_rows:, :] = grad
        grad = (
            got_ref[back, piece_rows : 2 * piece_rows, :]
            + got_ref[back, 2 * piece_rows : 2 * piece_rows + 1, :] * grad
        )
        return state, grad

    lax.fori_loop(0, count, lap, (zero, zero), unroll=8)


def local_kernel(
    act_ref, up_ref, write_ref, read_ref, shifted_ref, across_ref,
    back_ref, rows_ref, write_part_ref, read_part_ref, pair_sum, scores,
):
    bunch = pl.program_id(1)
    half = GROUP // 2
    triangle = lax.broadcasted_iota(jnp.int32, (half, half), 0) <= lax.broadcasted_iota(
        jnp.int32, (half, half), 1
    )

    @pl.when(bunch == 0)
    def _():
        scores[...] = dot_nt(write_ref[...], read_ref[...])
        pair_sum[...] = jnp.zeros_like(pair_sum)

    left = left_half(GROUP)
    for pair in range(BUNCH // 2):
        here = slice(pair * LANES, (pair + 1) * LANES)
        act = act_ref[:, here]
        up = up_ref[:, here]
        back_top = jnp.zeros((half, LANES), F32)
        back_low = jnp.zeros((half, LANES), F32)
        for side in range(2):
            head = 2 * pair + side
            keep = left if side == 0 else jnp.logical_not(left)
            act_one = jnp.where(keep, act, jnp.zeros_like(act))
            up_one = jnp.where(keep, up, jnp.zeros_like(up))
            late = across_ref[0, head : head + 1, :]
            soon = shifted_ref[0, :, head : head + 1]
            decay_a = jnp.where(triangle, jnp.exp2(late[:, :half] - soon[:half]), 0.0)
            decay_b = jnp.exp2(late[:, half:] - soon[:half])
            decay_c = jnp.where(triangle, jnp.exp2(late[:, half:] - soon[half:]), 0.0)
            decay_top = jnp.concatenate([decay_a, decay_b], axis=1)
            dots_top = dot_nt(act_one[:half], up)
            dots_low = dot_nt(act_one[half:], up[half:])
            pair_sum[:half, :] += decay_top * dots_top
            pair_sum[half:, half:] += decay_c * dots_low
            masked_top = (decay_top * scores[:half, :]).astype(BF16)
            masked_low = (decay_c * scores[half:, half:]).astype(BF16)
            sums = jnp.sum(masked_top.astype(F32) * dots_top, axis=0, keepdims=True)
            low_sums = jnp.sum(masked_low.astype(F32) * dots_low, axis=0, keepdims=True)
            rows_ref[0, head : head + 1, :half] = sums[:, :half]
            rows_ref[0, head : head + 1, half:] = sums[:, half:] + low_sums
            back_top += dot_nn(masked_top, up_one)
            back_low += dot_nn(masked_low, up_one[half:])
        back_ref[:half, here] = back_top
        back_ref[half:, here] = back_low

    @pl.when(bunch == pl.num_programs(1) - 1)
    def _():
        low = pair_sum[...].astype(BF16)
        write_part_ref[...] = dot_nn(low, read_ref[...])
        read_part_ref[...] = dot_tn(low, write_ref[...])


def cross_kernel(
    heads, piece_rows, act_ref, up_ref, back_ref, carried_ref, pieces_ref, early_ref, late_ref,
    out_ref, in_ref, spread_ref, write_ref, read_ref, rows_ref, write_part_ref, read_part_ref, dt_ref, scale_ref,
    act_grad_ref, log_ref, write_grad_ref, read_grad_ref, row_acc, col_acc, edge_acc,
):
    bunch = pl.program_id(0)
    rows = act_ref.shape[0]
    per_pair = LANES // piece_rows

    @pl.when(bunch == 0)
    def _():
        row_acc[...] = jnp.zeros_like(row_acc)
        col_acc[...] = jnp.zeros_like(col_acc)
        edge_acc[...] = jnp.zeros_like(edge_acc)
        write_grad_ref[...] = write_part_ref[...]
        read_grad_ref[...] = read_part_ref[...]

    left = left_half(GROUP)
    lane = lax.broadcasted_iota(jnp.int32, (GROUP, LANES), 1)
    enters, leaves = [[], []], [[], []]
    edges = [edge_acc[0:1, :], edge_acc[1:2, :]]
    lane_one = lax.broadcasted_iota(jnp.int32, (1, LANES), 1)
    for pair in range(BUNCH // 2):
        here = slice(pair * LANES, (pair + 1) * LANES)
        few = slice(pair * per_pair, (pair + 1) * per_pair)
        enter_0 = carried_ref[few, :piece_rows, :].reshape(LANES, LANES)
        leave_1 = carried_ref[few, piece_rows:, :].reshape(LANES, LANES)
        own = pieces_ref[few, :piece_rows, :].reshape(LANES, LANES)
        enter_1 = spread_ref[0:1, here] * enter_0 + early_ref[:, here]
        leave_0 = late_ref[:, here] + spread_ref[1:2, here] * leave_1
        end_1 = spread_ref[2:3, here] * enter_0 + own
        enters[0].append(enter_0.astype(BF16))
        enters[1].append(enter_1.astype(BF16))
        leaves[0].append(leave_0.astype(BF16))
        leaves[1].append(leave_1.astype(BF16))
        for block, product in enumerate((leave_0 * enter_1, leave_1 * end_1)):
            sums = jnp.sum(product, axis=0, keepdims=True)
            for side in range(2):
                keep = left[:1] if side == 0 else jnp.logical_not(left[:1])
                one = jnp.sum(jnp.where(keep, sums, 0.0), axis=1, keepdims=True)
                edges[block] = jnp.where(lane_one == bunch * BUNCH + 2 * pair + side, one, edges[block])
    edge_acc[0:1, :] = edges[0]
    edge_acc[1:2, :] = edges[1]
    for block in range(rows // GROUP):
        span = slice(block * GROUP, (block + 1) * GROUP)
        enter_low = jnp.concatenate(enters[block], axis=1)
        leave_low = jnp.concatenate(leaves[block], axis=1)
        offset = dot_nn(read_ref[span, :], enter_low)
        cross = dot_nn(write_ref[span, :], leave_low)
        act_scaled, up_scaled = [], []
        row_sums, col_sums = row_acc[span, :], col_acc[span, :]
        for pair in range(BUNCH // 2):
            here = slice(pair * LANES, (pair + 1) * LANES)
            act = act_ref[span, here].astype(F32)
            decay_out = pair_lanes(out_ref[0, span, :], pair)
            up_one = up_ref[span, here].astype(F32) * pair_lanes(in_ref[0, span, :], pair)
            up_scaled.append(up_one.astype(BF16))
            act_scaled.append((act * decay_out).astype(BF16))
            total = back_ref[span, here] + decay_out * cross[:, here]
            act_grad_ref[span, here] = total.astype(BF16)
            row_product = offset[:, here] * up_one
            col_product = act * total
            for side in range(2):
                keep = left if side == 0 else jnp.logical_not(left)
                place = lane == bunch * BUNCH + 2 * pair + side
                row_sums = jnp.where(
                    place, jnp.sum(jnp.where(keep, row_product, 0.0), axis=1, keepdims=True), row_sums
                )
                col_sums = jnp.where(
                    place, jnp.sum(jnp.where(keep, col_product, 0.0), axis=1, keepdims=True), col_sums
                )
        row_acc[span, :] = row_sums
        col_acc[span, :] = col_sums
        read_grad_ref[span, :] += dot_nt(jnp.concatenate(up_scaled, axis=1), enter_low)
        write_grad_ref[span, :] += dot_nt(jnp.concatenate(act_scaled, axis=1), leave_low)

    @pl.when(bunch == pl.num_programs(0) - 1)
    def _():
        table = order_table(GROUP, True).astype(BF16)
        for block in range(rows // GROUP):
            span = slice(block * GROUP, (block + 1) * GROUP)
            local_rows = rows_ref[:, :, span].reshape(heads, GROUP)
            padded = jnp.concatenate([local_rows, jnp.zeros((LANES - heads, GROUP), F32)], axis=0).T
            net = (padded + row_acc[span, :] - col_acc[span, :])[:, :heads]
            log_grad = exact_dot(table, net) + edge_acc[block : block + 1, :heads]
            decay = dt_ref[span, :] * scale_ref[...]
            log_ref[span, :] = col_acc[span, :heads] + decay * log_grad


def on_device(activation, step_size, decay_scale, write_vectors, read_vectors, upstream):
    rows, inner = activation.shape
    heads = decay_scale.shape[0]
    state = write_vectors.shape[1]
    count = lax.axis_size("seq")
    pairs = heads // 2
    piece_rows = pairs * state // count
    bunches = heads // BUNCH
    blocks = rows // GROUP
    wide = inner // bunches
    scale = decay_scale.reshape(1, heads)
    vmem = pl.BlockSpec(memory_space=pltpu.VMEM)
    hbm = pl.BlockSpec(memory_space=pl.ANY)
    columns = jax.ShapeDtypeStruct((bunches, rows, BUNCH), F32)
    across_shape = jax.ShapeDtypeStruct((bunches, BUNCH, rows), F32)

    pieces, early, late, shifted, decay_out, decay_in, across, spread = pl.pallas_call(
        partial(states_kernel, heads, piece_rows),
        name="states",
        in_specs=[vmem] * 4 + [hbm] * 2,
        out_specs=[hbm] * 3 + [vmem] * 5,
        out_shape=[
            jax.ShapeDtypeStruct((count, 2 * piece_rows + 8, LANES), F32),
            jax.ShapeDtypeStruct((state, inner), F32),
            jax.ShapeDtypeStruct((state, inner), F32),
            columns,
            columns,
            columns,
            across_shape,
            jax.ShapeDtypeStruct((8, inner), F32),
        ],
        scratch_shapes=[
            pltpu.VMEM((rows, inner), BF16),
            pltpu.VMEM((rows, inner), BF16),
            pltpu.VMEM((count, 2 * piece_rows + 8, LANES), F32),
            pltpu.VMEM((state, inner), F32),
            pltpu.VMEM((state, inner), F32),
            pltpu.SemaphoreType.DMA((bunches, 2)),
            pltpu.SemaphoreType.DMA((bunches, 3)),
        ],
        compiler_params=pltpu.CompilerParams(vmem_limit_bytes=40 * MIB),
        cost_estimate=pl.CostEstimate(flops=4 * rows * state * inner, bytes_accessed=8 * MIB, transcendentals=0),
    )(step_size, scale, write_vectors, read_vectors, activation, upstream)

    got = lax.all_to_all(pieces, "seq", 0, 0)

    back, local_rows, write_part, read_part = pl.pallas_call(
        local_kernel,
        name="local",
        grid=(blocks, bunches),
        in_specs=[
            pl.BlockSpec((GROUP, wide), lambda b, g: (b, g)),
            pl.BlockSpec((GROUP, wide), lambda b, g: (b, g)),
            pl.BlockSpec((GROUP, state), lambda b, g: (b, 0)),
            pl.BlockSpec((GROUP, state), lambda b, g: (b, 0)),
            pl.BlockSpec((1, GROUP, BUNCH), lambda b, g: (g, b, 0)),
            pl.BlockSpec((1, BUNCH, GROUP), lambda b, g: (g, 0, b)),
        ],
        out_specs=[
            pl.BlockSpec((GROUP, wide), lambda b, g: (b, g)),
            pl.BlockSpec((1, BUNCH, GROUP), lambda b, g: (g, 0, b)),
            pl.BlockSpec((GROUP, state), lambda b, g: (b, 0)),
            pl.BlockSpec((GROUP, state), lambda b, g: (b, 0)),
        ],
        out_shape=[
            jax.ShapeDtypeStruct((rows, inner), F32),
            across_shape,
            jax.ShapeDtypeStruct((rows, state), F32),
            jax.ShapeDtypeStruct((rows, state), F32),
        ],
        scratch_shapes=[pltpu.VMEM((GROUP, GROUP), F32), pltpu.VMEM((GROUP, GROUP), F32)],
        compiler_params=pltpu.CompilerParams(vmem_limit_bytes=24 * MIB),
        cost_estimate=pl.CostEstimate(
            flops=20_000_000_000, bytes_accessed=8 * MIB, transcendentals=blocks * heads * GROUP * GROUP
        ),
    )(activation, upstream, write_vectors, read_vectors, shifted, across)

    carried = pl.pallas_call(
        partial(scan_kernel, piece_rows),
        name="scan",
        in_specs=[vmem],
        out_specs=vmem,
        out_shape=jax.ShapeDtypeStruct((count, 2 * piece_rows, LANES), F32),
        compiler_params=pltpu.CompilerParams(vmem_limit_bytes=16 * MIB),
    )(got)
    carried = lax.all_to_all(carried, "seq", 0, 0)

    few = BUNCH // 2 * (LANES // piece_rows)
    whole = pl.BlockSpec((rows, state), lambda g: (0, 0))
    return pl.pallas_call(
        partial(cross_kernel, heads, piece_rows),
        name="cross",
        grid=(bunches,),
        in_specs=[
            pl.BlockSpec((rows, wide), lambda g: (0, g)),
            pl.BlockSpec((rows, wide), lambda g: (0, g)),
            pl.BlockSpec((rows, wide), lambda g: (0, g)),
            pl.BlockSpec((few, 2 * piece_rows, LANES), lambda g: (g, 0, 0)),
            pl.BlockSpec((few, 2 * piece_rows + 8, LANES), lambda g: (g, 0, 0)),
            pl.BlockSpec((state, wide), lambda g: (0, g)),
            pl.BlockSpec((state, wide), lambda g: (0, g)),
            pl.BlockSpec((1, rows, BUNCH), lambda g: (g, 0, 0)),
            pl.BlockSpec((1, rows, BUNCH), lambda g: (g, 0, 0)),
            pl.BlockSpec((8, wide), lambda g: (0, g)),
            whole,
            whole,
            pl.BlockSpec((bunches, BUNCH, rows), lambda g: (0, 0, 0)),
            whole,
            whole,
            pl.BlockSpec((rows, heads), lambda g: (0, 0)),
            pl.BlockSpec((1, heads), lambda g: (0, 0)),
        ],
        out_specs=[
            pl.BlockSpec((rows, wide), lambda g: (0, g)),
            pl.BlockSpec((rows, heads), lambda g: (0, 0)),
            whole,
            whole,
        ],
        out_shape=[
            jax.ShapeDtypeStruct((rows, inner), BF16),
            jax.ShapeDtypeStruct((rows, heads), F32),
            jax.ShapeDtypeStruct((rows, state), F32),
            jax.ShapeDtypeStruct((rows, state), F32),
        ],
        scratch_shapes=[
            pltpu.VMEM((rows, LANES), F32),
            pltpu.VMEM((rows, LANES), F32),
            pltpu.VMEM((8, LANES), F32),
        ],
        compiler_params=pltpu.CompilerParams(vmem_limit_bytes=32 * MIB),
        cost_estimate=pl.CostEstimate(flops=8 * rows * state * inner, bytes_accessed=16 * MIB, transcendentals=0),
    )(
        activation, upstream, back, carried, pieces, early, late, decay_out, decay_in, spread,
        write_vectors, read_vectors, local_rows, write_part, read_part, step_size, scale,
    )


def solution(mesh):
    spread = P(("dp", "seq"), None)
    return jax.shard_map(
        on_device,
        mesh=mesh,
        in_specs=(spread, spread, P("dp"), spread, spread, spread),
        out_specs=(spread, spread, spread, spread),
        check_vma=False,
    )
```

time: 1090 us -> 127 us (0.12)
  other arithmetic: 429 us -> 0 us
  local copies, waits for them, and re-layouts: 355 us -> 28.8 us
  blocking collectives: 178 us -> 44.4 us
  waiting for transfers between devices: 69.8 us -> 13.4 us
  Pallas kernels: 0 us -> 32.6 us
  matrix products: 28.8 us -> 0 us
  between operations: 14.4 us -> 0.78 us
    select_n x126 -> x0, other arithmetic: 412 us -> none  [lap(): jnp.where(position < mine, new, old)]
    dynamic_slice x260 -> x0, local copies, waits for them, and re-layouts: 248 us -> none  [the longest x252 241 us: lap(): longer = join(so_far, jax.tree.map(lambda part: part[position], pieces))]
    all_gather x1 -> x0, blocking collectives: 178 us -> none  [carried_in(): pieces = jax.tree.map(lambda part: lax.all_gather(part, axis), value)]
    all_gather x2 -> x0, waiting for transfers between devices: 69.8 us -> none  [carried_in(): pieces = jax.tree.map(lambda part: lax.all_gather(part, axis), value)]
    all_to_all x0 -> x1, blocking collectives: none -> 44.4 us  [on_device(): got = lax.all_to_all(pieces, 'seq', 0, 0)]
    rev x2 -> x0, local copies, waits for them, and re-layouts: 43.7 us -> none  [carried_in(): pieces = jax.tree.map(lambda part: part[::-1], pieces)]
    pallas_call x0 -> x4, Pallas kernels: none -> 32.6 us  [the longest x1 15.1 us: on_device(): pl.pallas_call(partial(cross_kernel, heads, piece_rows), name='cross', gr...]
    convert_element_type x4 -> x0, local copies, waits for them, and re-layouts: 29 us -> none  [the longest x2 15.5 us: on_device(): act_four * back_total]
  transfers between devices with their start and end apart: 2 -> 1, of which waited for: 1 -> 1; matrix products, arithmetic and copies ran while one was open for 34% -> 0% of each run, Pallas kernels for 0% -> 7%
where the time goes in v1:
time: 127 us; the launch traced here: 126 us
  blocking collectives  44.4 us (35%)
  Pallas kernels  32.6 us (26%)
  local copies, waits for them, and re-layouts  28.8 us (23%)
  waiting for transfers between devices  13.4 us (11%)
  starting transfers between devices  5.89 us (5%)
    all_to_all x1, blocking collectives, on_device(): got = lax.all_to_all(pieces, 'seq', 0, 0)  44.4 us
    unnamed x57, local copies, waits for them, and re-layouts  27.1 us
    pallas_call x1, Pallas kernels, on_device(): pl.pallas_call(partial(cross_kernel, heads, piece_rows), name='cross', gr...  15.1 us
    all_to_all x1, waiting for transfers between devices, on_device(): carried = lax.all_to_all(carried, 'seq', 0, 0)  13.4 us
    pallas_call x1, Pallas kernels, on_device(): pl.pallas_call(partial(states_kernel, heads, piece_rows), name='states',...  8.9 us
    pallas_call x1, Pallas kernels, on_device(): pl.pallas_call(local_kernel, name='local', grid=(blocks, bunches), in_spe...  8.35 us
    all_to_all x1, starting transfers between devices, on_device(): carried = lax.all_to_all(carried, 'seq', 0, 0)  5.89 us
  transfers between devices with their start and end apart: 1, of which 1 were waited for; matrix products, arithmetic and copies ran while one was open for 0% of the time, Pallas kernels for 7%

profile of v1, /device:TPU:0, one launch (start us, length us, event | category | flops | bytes accessed | tf_op | source)
XLA Modules:
  0.0 125.8 jit_solution(261979599316588715)
XLA Ops:
  0.6 1.0 copy.10.dt_ref
  1.6 0.0 copy-start.1
  1.6 1.6 %copy-done.1 = bf16[512,2048]{1,0:T(8,128)(2,1)S(1)} copy-done((bf16[512,2048]{1,0:T(8,128)(2,1)S(1)}, bf16[512,2048]{1,0:T(8,128)(2,1)}, u32[]{:S(2)}) %copy-start.1) | copy-done | bytes 2097176
  3.2 0.0 copy-start.4
  3.2 1.6 %copy-done.4 = bf16[512,2048]{1,0:T(8,128)(2,1)S(1)} copy-done((bf16[512,2048]{1,0:T(8,128)(2,1)S(1)}, bf16[512,2048]{1,0:T(8,128)(2,1)}, u32[]{:S(2)}) %copy-start.4) | copy-done | bytes 2097176
  4.8 0.0 copy-start.17
  4.8 0.9 copy-done.17
  5.7 0.0 copy-start.19
  5.7 0.9 copy-done.19
  6.6 0.0 copy-start.22
  6.6 0.7 copy-done.22
  7.3 8.9 %states.1 = (f32[64,72,128]{2,1,0:T(8,128)S(1)}, f32[128,2048]{1,0:T(8,128)S(1)}, f32[128,2048]{1,0:T(8,128)S(1)}, f32[4,512,8]{2,1,0:T(8,128)S(1)}, f32[4,512,8...) custom-call(f32[512,32]{1,0:T(8,128)S(1)} %copy.10.dt_ref, ...), custom_call_target="tpu_custom_call" | custom-call | flops 536870912 | bytes 8388608 | tf_op jit(solution)/shard_map/states/pallas_call | solution.py:339
  16.2 0.0 copy-start.24
  16.2 1.0 copy-done.24
  17.1 0.0 copy-start.9
  17.1 0.0 copy-start.11
  17.1 0.0 copy-start.13
  17.1 0.0 copy-start.15
  17.2 0.0 copy-start.26
  17.2 44.4 %all_to_all.10.got_ref = f32[64,72,128]{2,1,0:T(8,128)S(1)} all-to-all(f32[64,72,128]{2,1,0:T(8,128)S(1)} %get-tuple-element.19.pieces_ref), channel_id=1, replica_groups=mesh['seq'=64,'dp'=2] {'seq'}, dimensions={0} | all-to-all | bytes 4718592 | tf_op jit(solution)/shard_map/all_to_all | solution.py:367
  61.5 0.0 copy-done.9
  61.5 0.0 copy-done.11
  61.5 0.0 copy-done.13
  61.5 0.0 copy-done.15
  61.5 0.0 copy-done.26
  61.6 0.3 scan.1
  61.8 0.0 copy-start
  61.8 1.3 %copy-done = f32[64,64,128]{2,1,0:T(8,128)} copy-done((f32[64,64,128]{2,1,0:T(8,128)}, f32[64,64,128]{2,1,0:T(8,128)S(1)}, u32[]{:S(2)}) %copy-start) | copy-done | bytes 2097176
  63.1 0.0 copy-start.18
  63.1 0.0 copy-start.20
  63.1 5.9 %all-to-all-start.1 = ((f32[64,64,128]{2,1,0:T(8,128)}), f32[64,64,128]{2,1,0:T(8,128)}, u32[]{:S(2)}, u32[]{:S(2)}) async-start(f32[64,64,128]{2,1,0:T(8,128)} %copy-done), calls=%async_computation.1 | async-start | bytes 4194304 | tf_op jit(solution)/shard_map/all_to_all | solution.py:408
  69.0 0.0 copy-done.18
  69.1 0.0 copy-done.20
  69.1 0.0 copy-start.2
  69.1 1.6 %copy-done.2 = bf16[512,2048]{1,0:T(8,128)(2,1)S(1)} copy-done((bf16[512,2048]{1,0:T(8,128)(2,1)S(1)}, bf16[512,2048]{1,0:T(8,128)(2,1)}, u32[]{:S(2)}) %copy-start.2) | copy-done | bytes 2097176
  70.7 0.0 copy-start.5
  70.7 1.6 %copy-done.5 = bf16[512,2048]{1,0:T(8,128)(2,1)S(1)} copy-done((bf16[512,2048]{1,0:T(8,128)(2,1)S(1)}, bf16[512,2048]{1,0:T(8,128)(2,1)}, u32[]{:S(2)}) %copy-start.5) | copy-done | bytes 2097176
  72.2 0.0 copy-start.25
  72.3 1.2 copy-done.25
  73.5 0.0 copy-start.27
  73.5 0.8 copy-done.27
  74.3 0.0 copy-start.23
  74.3 8.3 %local.1 = (f32[512,2048]{1,0:T(8,128)S(1)}, f32[4,8,512]{2,1,0:T(8,128)S(1)}, f32[512,128]{1,0:T(8,128)S(1)}, f32[512,128]{1,0:T(8,128)S(1)}) custom-call(bf16[512,2048]{1,0:T(8,128)(2,1)S(1)} %copy-done.2, bf16[512,2048]{1,0:T(8,128)(2,1)S(1)} %copy-done.5, bf16[512,128]{1,0:T(8,128)(2,1)S(1)} %copy-done.18, bf16[512,128]{1,0:T(8,128)(2,1)S(1)} %copy-done.20, ...), custom_call_target="tpu_custom_call" | custom-call | flops 20000000000 | bytes 8388608 | tf_op jit(solution)/shard_map/local/pallas_call | solution.py:369
  82.7 0.0 copy-start.7
  82.7 2.0 %copy-done.7 = f32[512,2048]{1,0:T(8,128)} copy-done((f32[512,2048]{1,0:T(8,128)}, f32[512,2048]{1,0:T(8,128)S(1)}, u32[]{:S(2)}) %copy-start.7) | copy-done | bytes 4194328
  84.6 13.4 %all-to-all-done.1.carried_ref = f32[64,64,128]{2,1,0:T(8,128)} async-done(((f32[64,64,128]{2,1,0:T(8,128)}), f32[64,64,128]{2,1,0:T(8,128)}, u32[]{:S(2)}, u32[]{:S(2)}) %all-to-all-start.1) | async-done | bytes 2097184 | tf_op jit(solution)/shard_map/all_to_all | solution.py:408
  98.1 0.0 copy-done.23
  98.1 0.0 copy-start.3
  98.1 1.6 %copy-done.3 = bf16[512,2048]{1,0:T(8,128)(2,1)S(1)} copy-done((bf16[512,2048]{1,0:T(8,128)(2,1)S(1)}, bf16[512,2048]{1,0:T(8,128)(2,1)}, u32[]{:S(2)}) %copy-start.3) | copy-done | bytes 2097176
  99.7 0.0 copy-start.6
  99.7 1.6 %copy-done.6 = bf16[512,2048]{1,0:T(8,128)(2,1)S(1)} copy-done((bf16[512,2048]{1,0:T(8,128)(2,1)S(1)}, bf16[512,2048]{1,0:T(8,128)(2,1)}, u32[]{:S(2)}) %copy-start.6) | copy-done | bytes 2097176
  101.3 0.0 copy-start.8
  101.3 2.2 %copy-done.8 = f32[512,2048]{1,0:T(8,128)S(1)} copy-done((f32[512,2048]{1,0:T(8,128)S(1)}, f32[512,2048]{1,0:T(8,128)}, u32[]{:S(2)}) %copy-start.8) | copy-done | bytes 4194328
  103.5 0.0 copy-start.10
  103.5 1.2 copy-done.10
  104.7 0.0 copy-start.12
  104.7 1.2 copy-done.12
  105.9 0.0 copy-start.14
  105.9 1.2 copy-done.14
  107.1 1.2 copy-done.16
  108.4 15.1 %cross.1 = (bf16[512,2048]{1,0:T(8,128)(2,1)}, f32[512,32]{1,0:T(8,128)S(1)}, f32[512,128]{1,0:T(8,128)}, f32[512,128]{1,0:T(8,128)}) custom-call(bf16[512,2048]{1,0:T(8,128)(2,1)S(1)} %copy-done.3, bf16[512,2048]{1,0:T(8,128)(2,1)S(1)} %copy-done.6, f32[512,2048]{1,0:T(8,128)S(1)} %copy-done.8, f32[64,64,128]{2,1,0:T(8,128)} %all-to-all-done.1.carried_ref, ...), custom_call_target="tpu_custom_call" | custom-call | flops 1073741824 | bytes 16777216 | tf_op jit(solution)/shard_map/cross/pallas_call | solution.py:412
  123.5 0.0 copy-start.21
  123.5 0.7 copy-done.21
  124.2 1.7 %copy.12 = f32[512,32]{0,1:T(8,128)} copy(f32[512,32]{1,0:T(8,128)} %copy-done.21) | data formatting | bytes 131072 | tf_op jit(solution)/shard_map/cross/pallas_call | solution.py:412
  (1 shorter events, 0.0 us)
Async XLA Ops:
  1.6 1.6 %copy-start.1 = (bf16[512,2048]{1,0:T(8,128)(2,1)S(1)}, bf16[512,2048]{1,0:T(8,128)(2,1)}, u32[]{:S(2)}) copy-start(bf16[512,2048]{1,0:T(8,128)(2,1)} %act_ref.5) | copy-start | bytes 6291460
  3.2 1.6 %copy-start.4 = (bf16[512,2048]{1,0:T(8,128)(2,1)S(1)}, bf16[512,2048]{1,0:T(8,128)(2,1)}, u32[]{:S(2)}) copy-start(bf16[512,2048]{1,0:T(8,128)(2,1)} %up_ref.5) | copy-start | bytes 6291460
  4.8 0.9 copy-start.17
  5.7 0.9 copy-start.19
  6.6 0.7 copy-start.22
  16.2 1.0 copy-start.24
  17.1 44.4 %copy-start.9 = (f32[128,2048]{1,0:T(8,128)}, f32[128,2048]{1,0:T(8,128)S(1)}, u32[]{:S(2)}) copy-start(f32[128,2048]{1,0:T(8,128)S(1)} %get-tuple-element.20.early_ref) | copy-start | bytes 3145732
  17.1 44.4 %copy-start.11 = (f32[128,2048]{1,0:T(8,128)}, f32[128,2048]{1,0:T(8,128)S(1)}, u32[]{:S(2)}) copy-start(f32[128,2048]{1,0:T(8,128)S(1)} %get-tuple-element.21.late_ref) | copy-start | bytes 3145732
  17.1 44.4 %copy-start.13 = (f32[4,512,8]{2,1,0:T(8,128)}, f32[4,512,8]{2,1,0:T(8,128)S(1)}, u32[]{:S(2)}) copy-start(f32[4,512,8]{2,1,0:T(8,128)S(1)} %get-tuple-element.22.out_ref) | copy-start | bytes 196612
  17.1 44.4 %copy-start.15 = (f32[4,512,8]{2,1,0:T(8,128)}, f32[4,512,8]{2,1,0:T(8,128)S(1)}, u32[]{:S(2)}) copy-start(f32[4,512,8]{2,1,0:T(8,128)S(1)} %get-tuple-element.23.in_ref) | copy-start | bytes 196612
  17.2 44.4 %copy-start.26 = (f32[4,8,512]{2,1,0:T(8,128)}, f32[4,8,512]{2,1,0:T(8,128)S(1)}, u32[]{:S(2)}) copy-start(f32[4,8,512]{2,1,0:T(8,128)S(1)} %get-tuple-element.17.across_ref) | copy-start | bytes 196612
  61.8 1.3 %copy-start = (f32[64,64,128]{2,1,0:T(8,128)}, f32[64,64,128]{2,1,0:T(8,128)S(1)}, u32[]{:S(2)}) copy-start(f32[64,64,128]{2,1,0:T(8,128)S(1)} %scan.1) | copy-start | bytes 6291460
  63.1 5.9 %copy-start.18 = (bf16[512,128]{1,0:T(8,128)(2,1)S(1)}, bf16[512,128]{1,0:T(8,128)(2,1)}, u32[]{:S(2)}) copy-start(bf16[512,128]{1,0:T(8,128)(2,1)} %write_ref.5) | copy-start | bytes 393220
  63.1 5.9 %copy-start.20 = (bf16[512,128]{1,0:T(8,128)(2,1)S(1)}, bf16[512,128]{1,0:T(8,128)(2,1)}, u32[]{:S(2)}) copy-start(bf16[512,128]{1,0:T(8,128)(2,1)} %read_ref.5) | copy-start | bytes 393220
  63.1 34.9 %all-to-all-start.1 = ((f32[64,64,128]{2,1,0:T(8,128)}), f32[64,64,128]{2,1,0:T(8,128)}, u32[]{:S(2)}, u32[]{:S(2)}) async-start(f32[64,64,128]{2,1,0:T(8,128)} %copy-done), calls=%async_computation.1 | async-start | bytes 4194304 | tf_op jit(solution)/shard_map/all_to_all | solution.py:408
  69.1 1.6 %copy-start.2 = (bf16[512,2048]{1,0:T(8,128)(2,1)S(1)}, bf16[512,2048]{1,0:T(8,128)(2,1)}, u32[]{:S(2)}) copy-start(bf16[512,2048]{1,0:T(8,128)(2,1)} %act_ref.5) | copy-start | bytes 6291460
  70.7 1.6 %copy-start.5 = (bf16[512,2048]{1,0:T(8,128)(2,1)S(1)}, bf16[512,2048]{1,0:T(8,128)(2,1)}, u32[]{:S(2)}) copy-start(bf16[512,2048]{1,0:T(8,128)(2,1)} %up_ref.5) | copy-start | bytes 6291460
  72.2 1.2 copy-start.25
  73.5 0.8 copy-start.27
  74.3 23.8 %copy-start.23 = (f32[32]{0:T(128)S(1)}, f32[32]{0:T(128)}, u32[]{:S(2)}) copy-start(f32[32]{0:T(128)} %param.8) | copy-start | bytes 388
  82.7 2.0 %copy-start.7 = (f32[512,2048]{1,0:T(8,128)}, f32[512,2048]{1,0:T(8,128)S(1)}, u32[]{:S(2)}) copy-start(f32[512,2048]{1,0:T(8,128)S(1)} %get-tuple-element.18.back_ref) | copy-start | bytes 12582916
  98.1 1.6 %copy-start.3 = (bf16[512,2048]{1,0:T(8,128)(2,1)S(1)}, bf16[512,2048]{1,0:T(8,128)(2,1)}, u32[]{:S(2)}) copy-start(bf16[512,2048]{1,0:T(8,128)(2,1)} %act_ref.5) | copy-start | bytes 6291460
  99.7 1.6 %copy-start.6 = (bf16[512,2048]{1,0:T(8,128)(2,1)S(1)}, bf16[512,2048]{1,0:T(8,128)(2,1)}, u32[]{:S(2)}) copy-start(bf16[512,2048]{1,0:T(8,128)(2,1)} %up_ref.5) | copy-start | bytes 6291460
  101.3 2.2 %copy-start.8 = (f32[512,2048]{1,0:T(8,128)S(1)}, f32[512,2048]{1,0:T(8,128)}, u32[]{:S(2)}) copy-start(f32[512,2048]{1,0:T(8,128)} %copy-done.7) | copy-start | bytes 12582916
  103.5 1.2 copy-start.10
  104.7 1.2 copy-start.12
  105.9 1.2 copy-start.14
  107.1 1.2 copy-start.16
  123.5 0.7 copy-start.21

commit v2 on v1

v2 whole, which is shorter than its diff:
```python
import math
from functools import partial

import jax
import jax.numpy as jnp
from jax import lax
from jax.experimental import pallas as pl
from jax.experimental.pallas import tpu as pltpu
from jax.sharding import PartitionSpec as P

GROUP = 256
LANES = 128
BUNCH = 8
LOG2E = math.log2(math.e)
F32 = jnp.float32
BF16 = jnp.bfloat16
MIB = 1 << 20
VMEM_LIMIT = 56 * MIB
AHEAD = 4


def dot_nn(a, b):
    return jnp.dot(a, b, preferred_element_type=F32)


def dot_nt(a, b):
    return lax.dot_general(a, b, (((1,), (1,)), ((), ())), preferred_element_type=F32)


def dot_tn(a, b):
    return lax.dot_general(a, b, (((0,), (0,)), ((), ())), preferred_element_type=F32)


def split(value, terms):
    parts = []
    for _ in range(terms):
        part = value.astype(BF16)
        parts.append(part)
        value = value - part.astype(F32)
    return jnp.concatenate(parts, axis=0)


def exact_dot(value, table):
    rows = value.shape[0]
    product = dot_nn(split(value, 3), table)
    return product[:rows] + product[rows : 2 * rows] + product[2 * rows :]


def left_half(rows):
    return lax.broadcasted_iota(jnp.int32, (rows, LANES), 1) < LANES // 2


def order_table(size, upper):
    row = lax.broadcasted_iota(jnp.int32, (size, size), 0)
    column = lax.broadcasted_iota(jnp.int32, (size, size), 1)
    return jnp.where(row <= column if upper else row >= column, 1.0, 0.0).astype(BF16)


def channel_table(heads, width):
    head = lax.broadcasted_iota(jnp.int32, (heads, width), 0)
    lane = lax.broadcasted_iota(jnp.int32, (heads, width), 1)
    return jnp.where(lane // (width // heads) == head, 1.0, 0.0)


def spread_heads(across, table):
    return dot_tn(split(across, 2), jnp.concatenate([table, table], axis=0))


def states_kernel(
    heads, piece_rows, dt_ref, scale_ref, write_ref, read_ref, act_ref, up_ref,
    pieces_ref, tables_ref, spread_hbm_ref, dt_buf, write_buf, read_buf, act_buf, up_buf, piece_buf, across_ref, spread_ref,
    in_sems, small_sems, out_sems,
):
    rows = dt_ref.shape[1]
    blocks = rows // GROUP
    bunches = heads // BUNCH
    wide = BUNCH // 2 * LANES
    small = [
        pltpu.make_async_copy(source, target, small_sems.at[which])
        for which, (source, target) in enumerate(
            ((dt_ref, dt_buf), (write_ref, write_buf), (read_ref, read_buf), (across_ref, tables_ref), (spread_ref, spread_hbm_ref))
        )
    ]
    loads = []
    for bunch in range(bunches):
        for which, (source, target) in enumerate(((act_ref, act_buf), (up_ref, up_buf))):
            lanes = pl.ds(bunch * wide, wide)
            loads.append(
                pltpu.make_async_copy(
                    source.at[:, lanes], target.at[:, lanes], in_sems.at[bunch, which]
                )
            )
    small[0].start()
    for copy in loads[:AHEAD]:
        copy.start()
    small[1].start()
    small[2].start()
    small[0].wait()
    same = lax.broadcasted_iota(jnp.int32, (heads, heads), 0) == lax.broadcasted_iota(
        jnp.int32, (heads, heads), 1
    )
    scale = jnp.sum(jnp.where(same, scale_ref[...], 0.0), axis=1, keepdims=True)
    dt = dt_buf[...]
    log_decay = dt * scale
    across_ref[4 * heads :, :] = log_decay
    order = order_table(GROUP, True)
    stacked = jnp.concatenate([log_decay[:, b * GROUP : (b + 1) * GROUP] for b in range(blocks)], axis=0)
    running = exact_dot(stacked, order)
    totals = running[:, GROUP - 1 : GROUP]
    entering = jnp.exp(running)
    leaving = jnp.exp(totals - running)
    for block in range(blocks):
        span = slice(block * GROUP, (block + 1) * GROUP)
        some = slice(block * heads, (block + 1) * heads)
        across_ref[:heads, span] = running[some] * LOG2E
        across_ref[heads : 2 * heads, span] = running[some] * LOG2E - jnp.log2(dt[:, span])
        across_ref[2 * heads : 3 * heads, span] = leaving[some] * dt[:, span]
        across_ref[3 * heads : 4 * heads, span] = entering[some]
    small[3].start()
    first_total, second_total = totals[:heads], totals[heads:]
    first_running, second_running = running[:heads], running[heads:] + first_total
    device_total = first_total + second_total
    device_in = jnp.concatenate([entering[:heads], jnp.exp(second_running)], axis=1)
    device_out = dt * jnp.concatenate(
        [jnp.exp(device_total - first_running), leaving[heads:]], axis=1
    )
    columns = [jnp.exp(first_total), jnp.exp(second_total), jnp.exp(device_total)]
    table = channel_table(BUNCH, wide)
    table_low = table.astype(BF16)
    for bunch in range(bunches):
        lanes = slice(bunch * wide, (bunch + 1) * wide)
        some = slice(bunch * BUNCH, (bunch + 1) * BUNCH)
        first, second, both = (
            jnp.sum(table * column[some], axis=0, keepdims=True) for column in columns
        )
        spread_ref[:, lanes] = jnp.concatenate([first, second, both, jnp.zeros((5, wide), F32)], axis=0)
    small[4].start()
    small[1].wait()
    write_across = write_buf[...].T
    small[2].wait()
    read_across = read_buf[...].T
    per_pair = LANES // piece_rows
    stores = []
    for bunch in range(bunches):
        lanes = slice(bunch * wide, (bunch + 1) * wide)
        some = slice(bunch * BUNCH, (bunch + 1) * BUNCH)
        both = spread_ref[2:3, lanes]
        loads[2 * bunch].wait()
        if 2 * bunch + AHEAD < len(loads):
            loads[2 * bunch + AHEAD].start()
        act_scaled = act_buf[:, lanes].astype(F32) * spread_heads(device_out[some], table_low)
        state = dot_nn(write_across, act_scaled.astype(BF16))
        loads[2 * bunch + 1].wait()
        if 2 * bunch + 1 + AHEAD < len(loads):
            loads[2 * bunch + 1 + AHEAD].start()
        up_scaled = up_buf[:, lanes].astype(F32) * spread_heads(device_in[some], table_low)
        grad = dot_nn(read_across, up_scaled.astype(BF16))
        for local in range(BUNCH // 2):
            pair = bunch * BUNCH // 2 + local
            here = slice(local * LANES, (local + 1) * LANES)
            few = slice(pair * per_pair, (pair + 1) * per_pair)
            piece_buf[few, :piece_rows, :] = state[:, here].reshape(per_pair, piece_rows, LANES)
            piece_buf[few, piece_rows : 2 * piece_rows, :] = grad[:, here].reshape(
                per_pair, piece_rows, LANES
            )
            piece_buf[few, 2 * piece_rows :, :] = jnp.broadcast_to(
                both[:, here][None], (per_pair, 8, LANES)
            )
        few = pl.ds(bunch * BUNCH // 2 * per_pair, BUNCH // 2 * per_pair)
        copy = pltpu.make_async_copy(piece_buf.at[few], pieces_ref.at[few], out_sems.at[bunch])
        copy.start()
        stores.append(copy)
    for copy in stores + small[3:]:
        copy.wait()


def scan_kernel(piece_rows, got_ref, after_ref, carried_ref):
    count = got_ref.shape[0]
    zero = jnp.zeros((piece_rows, LANES), F32)

    def lap(step, carry):
        state, grad = carry
        carried_ref[step, :piece_rows, :] = state
        state = got_ref[step, 2 * piece_rows : 2 * piece_rows + 1, :] * state + got_ref[step, :piece_rows, :]
        back = count - 1 - step
        carried_ref[back, piece_rows:, :] = grad
        grad = (
            got_ref[back, piece_rows : 2 * piece_rows, :]
            + got_ref[back, 2 * piece_rows : 2 * piece_rows + 1, :] * grad
        )
        return state, grad

    lax.fori_loop(0, count, lap, (zero, zero), unroll=8)


def local_kernel(
    act_ref, up_ref, write_ref, read_ref, running_ref, shifted_ref, out_ref, in_ref,
    back_ref, act_scaled_ref, up_scaled_ref, inside_ref, rows_ref, columns_ref, write_part_ref, read_part_ref, done_ref,
    pair_sum, scores,
):
    bunch = pl.program_id(1)
    half = GROUP // 2
    wide = act_ref.shape[1]
    triangle = lax.broadcasted_iota(jnp.int32, (half, half), 0) <= lax.broadcasted_iota(
        jnp.int32, (half, half), 1
    )

    @pl.when(bunch == 0)
    def _():
        scores[...] = dot_nt(write_ref[...], read_ref[...])
        pair_sum[...] = jnp.zeros_like(pair_sum)

    table = channel_table(BUNCH, wide).astype(BF16)
    act_scaled = (act_ref[...].astype(F32) * spread_heads(out_ref[...], table)).astype(BF16)
    up_scaled = (up_ref[...].astype(F32) * spread_heads(in_ref[...], table)).astype(BF16)
    act_scaled_ref[...] = act_scaled
    up_scaled_ref[...] = up_scaled

    @pl.when(pl.program_id(0) == 0)
    def _():
        inside_ref[0] = dot_tn(write_ref[...], act_scaled)

    @pl.when(pl.program_id(0) == 1)
    def _():
        inside_ref[0] = dot_tn(read_ref[...], up_scaled)

    shifted = jnp.concatenate([shifted_ref[...], jnp.zeros((LANES - BUNCH, GROUP), F32)], axis=0).T
    left = left_half(GROUP)
    lane = lax.broadcasted_iota(jnp.int32, (GROUP, LANES), 1)
    columns = jnp.zeros((GROUP, LANES), F32)
    for pair in range(BUNCH // 2):
        here = slice(pair * LANES, (pair + 1) * LANES)
        act = act_ref[:, here]
        up = up_ref[:, here]
        back_top = jnp.zeros((half, LANES), F32)
        back_low = jnp.zeros((half, LANES), F32)
        for side in range(2):
            head = 2 * pair + side
            keep = left if side == 0 else jnp.logical_not(left)
            act_one = jnp.where(keep, act, jnp.zeros_like(act))
            up_one = jnp.where(keep, up, jnp.zeros_like(up))
            late = running_ref[head : head + 1, :]
            soon = shifted[:, head : head + 1]
            decay_a = jnp.where(triangle, jnp.exp2(late[:, :half] - soon[:half]), 0.0)
            decay_b = jnp.exp2(late[:, half:] - soon[:half])
            decay_c = jnp.where(triangle, jnp.exp2(late[:, half:] - soon[half:]), 0.0)
            decay_top = jnp.concatenate([decay_a, decay_b], axis=1)
            dots_top = dot_nt(act_one[:half], up)
            dots_low = dot_nt(act_one[half:], up[half:])
            pair_sum[:half, :] += decay_top * dots_top
            pair_sum[half:, half:] += decay_c * dots_low
            masked_top = (decay_top * scores[:half, :]).astype(BF16)
            masked_low = (decay_c * scores[half:, half:]).astype(BF16)
            sums = jnp.sum(masked_top.astype(F32) * dots_top, axis=0, keepdims=True)
            low_sums = jnp.sum(masked_low.astype(F32) * dots_low, axis=0, keepdims=True)
            rows_ref[head : head + 1, :half] = sums[:, :half]
            rows_ref[head : head + 1, half:] = sums[:, half:] + low_sums
            back_top += dot_nn(masked_top, up_one)
            back_low += dot_nn(masked_low, up_one[half:])
        back = jnp.concatenate([back_top, back_low], axis=0)
        back_ref[:, here] = back.astype(BF16)
        product = act.astype(F32) * back
        for side in range(2):
            keep = left if side == 0 else jnp.logical_not(left)
            one = jnp.sum(jnp.where(keep, product, 0.0), axis=1, keepdims=True)
            columns = jnp.where(lane == 2 * pair + side, one, columns)
    columns_ref[...] = columns.T[:BUNCH]

    @pl.when(bunch == pl.num_programs(1) - 1)
    def _():
        low = pair_sum[...].astype(BF16)
        done_ref[...] = jnp.zeros_like(done_ref)
        write_part_ref[...] = dot_nn(low, read_ref[...])
        read_part_ref[...] = dot_tn(low, write_ref[...])


def halves(value):
    high = value.astype(BF16)
    return [high, (value - high.astype(F32)).astype(BF16)]


def cross_kernel(
    heads, piece_rows, act_scaled_ref, up_scaled_ref, back_ref, carried_ref, inside_ref, tables_ref, spread_ref,
    rows_ref, columns_ref, write_ref, read_ref, write_part_ref, read_part_ref,
    act_grad_ref, log_ref, write_grad_ref, read_grad_ref, act_grad_buf, sems,
):
    rows, inner = act_scaled_ref.shape
    blocks = rows // GROUP
    bunches = heads // BUNCH
    wide = inner // bunches
    per_pair = LANES // piece_rows

    def gather(low, bunch):
        return jnp.concatenate(
            [
                carried_ref[pair * per_pair : (pair + 1) * per_pair, low : low + piece_rows, :].reshape(
                    LANES, LANES
                )
                for pair in range(bunch * wide // LANES, (bunch + 1) * wide // LANES)
            ],
            axis=1,
        )

    table = channel_table(BUNCH, wide)
    table_low = table.astype(BF16)
    channel = lax.broadcasted_iota(jnp.int32, (2 * BUNCH, 4 * wide), 1)
    lane = lax.broadcasted_iota(jnp.int32, (2 * BUNCH, 4 * wide), 0)
    place = channel // (2 * wide) * BUNCH + channel % wide // (wide // BUNCH)
    gather_table = jnp.where(lane == place, 1.0, 0.0).astype(BF16)
    order = order_table(GROUP, False)
    copies = []
    for bunch in range(bunches):
        lanes = slice(bunch * wide, (bunch + 1) * wide)
        some = slice(bunch * BUNCH, (bunch + 1) * BUNCH)
        first, second = spread_ref[0:1, lanes], spread_ref[1:2, lanes]
        enter_0, leave_1 = gather(0, bunch), gather(piece_rows, bunch)
        kept_0, kept_1 = first * enter_0, second * leave_1
        enter_1 = kept_0 + inside_ref[0, :, lanes]
        leave_0 = inside_ref[1, :, lanes] + kept_1
        enters, leaves = (enter_0, enter_1), (leave_0, leave_1)
        edges = [
            jnp.sum(table * jnp.sum(product, axis=0, keepdims=True), axis=1, keepdims=True)
            for product in (leave_0 * kept_0, kept_1 * enter_1)
        ]
        nets, cols = [], []
        for block in range(blocks):
            span = slice(block * GROUP, (block + 1) * GROUP)
            enter_low = enters[block].astype(BF16)
            leave_low = leaves[block].astype(BF16)
            offset = dot_nn(read_ref[span, :], enter_low)
            cross = dot_nn(write_ref[span, :], leave_low)
            decay_out = spread_heads(tables_ref[2 * heads + bunch * BUNCH : 2 * heads + (bunch + 1) * BUNCH, span], table_low)
            act_grad_buf[span, lanes] = (back_ref[span, lanes].astype(F32) + decay_out * cross).astype(BF16)
            act_scaled, up_scaled = act_scaled_ref[span, lanes], up_scaled_ref[span, lanes]
            row_products = offset * up_scaled.astype(F32)
            col_products = cross * act_scaled.astype(F32)
            sums = dot_nt(
                gather_table, jnp.concatenate(halves(row_products) + halves(col_products), axis=1)
            )
            column = columns_ref[some, span] + sums[BUNCH:]
            nets.append(rows_ref[some, span] + sums[:BUNCH] - column)
            cols.append(column)
            edges[block] += jnp.sum(sums[BUNCH:], axis=1, keepdims=True)
            read_cross = dot_nt(up_scaled, enter_low)
            write_cross = dot_nt(act_scaled, leave_low)
            if bunch == 0:
                read_grad_ref[span, :] = read_part_ref[span, :] + read_cross
                write_grad_ref[span, :] = write_part_ref[span, :] + write_cross
            else:
                read_grad_ref[span, :] += read_cross
                write_grad_ref[span, :] += write_cross
        few = pl.ds(bunch * wide, wide)
        copy = pltpu.make_async_copy(act_grad_buf.at[:, few], act_grad_ref.at[:, few], sems.at[bunch])
        copy.start()
        copies.append(copy)
        suffix = exact_dot(jnp.concatenate(nets, axis=0), order)
        for block in range(blocks):
            span = slice(block * GROUP, (block + 1) * GROUP)
            log_grad = suffix[block * BUNCH : (block + 1) * BUNCH] + edges[block]
            log_ref[some, span] = cols[block] + tables_ref[4 * heads + bunch * BUNCH : 4 * heads + (bunch + 1) * BUNCH, span] * log_grad
    for copy in copies:
        copy.wait()


def on_device(activation, step_size, decay_scale, write_vectors, read_vectors, upstream):
    rows, inner = activation.shape
    heads = decay_scale.shape[0]
    state = write_vectors.shape[1]
    count = lax.axis_size("seq")
    pairs = heads // 2
    piece_rows = pairs * state // count
    bunches = heads // BUNCH
    blocks = rows // GROUP
    wide = inner // bunches
    scale = decay_scale.reshape(1, heads)
    vmem = pl.BlockSpec(memory_space=pltpu.VMEM)
    hbm = pl.BlockSpec(memory_space=pl.ANY)
    across = jax.ShapeDtypeStruct((heads, rows), F32)
    low = jax.ShapeDtypeStruct((rows, inner), BF16)
    part = jax.ShapeDtypeStruct((rows, state), F32)

    pieces, tables, spread = pl.pallas_call(
        partial(states_kernel, heads, piece_rows),
        name="states",
        in_specs=[hbm, vmem] + [hbm] * 4,
        out_specs=[hbm] * 3,
        out_shape=[
            jax.ShapeDtypeStruct((count, 2 * piece_rows + 8, LANES), F32),
            jax.ShapeDtypeStruct((5 * heads, rows), F32),
            jax.ShapeDtypeStruct((8, inner), F32),
        ],
        scratch_shapes=[
            pltpu.VMEM((heads, rows), F32),
            pltpu.VMEM((rows, state), BF16),
            pltpu.VMEM((rows, state), BF16),
            pltpu.VMEM((rows, inner), BF16),
            pltpu.VMEM((rows, inner), BF16),
            pltpu.VMEM((count, 2 * piece_rows + 8, LANES), F32),
            pltpu.VMEM((5 * heads, rows), F32),
            pltpu.VMEM((8, inner), F32),
            pltpu.SemaphoreType.DMA((bunches, 2)),
            pltpu.SemaphoreType.DMA((5,)),
            pltpu.SemaphoreType.DMA((bunches,)),
        ],
        compiler_params=pltpu.CompilerParams(vmem_limit_bytes=VMEM_LIMIT),
        cost_estimate=pl.CostEstimate(flops=4 * rows * state * inner, bytes_accessed=8 * MIB, transcendentals=0),
    )(step_size.T, scale, write_vectors, read_vectors, activation, upstream)

    got = lax.all_to_all(pieces, "seq", 0, 0)

    narrow = pl.BlockSpec((BUNCH, GROUP), lambda b, g: (g, b))
    def table(which):
        return pl.BlockSpec((BUNCH, GROUP), lambda b, g: (which * bunches + g, b))

    block_wide = pl.BlockSpec((GROUP, wide), lambda b, g: (b, g))
    block_state = pl.BlockSpec((GROUP, state), lambda b, g: (b, 0))
    back, act_scaled, up_scaled, inside, local_rows, local_columns, write_part, read_part, done = pl.pallas_call(
        local_kernel,
        name="local",
        grid=(blocks, bunches),
        in_specs=[block_wide, block_wide, block_state, block_state] + [table(i) for i in range(4)],
        out_specs=[
            block_wide,
            block_wide,
            block_wide,
            pl.BlockSpec((1, state, wide), lambda b, g: (b, 0, g)),
            narrow,
            narrow,
            block_state,
            block_state,
            pl.BlockSpec((8, LANES), lambda b, g: (0, 0)),
        ],
        out_shape=[low, low, low, jax.ShapeDtypeStruct((blocks, state, inner), F32), across, across, part, part, jax.ShapeDtypeStruct((8, LANES), F32)],
        scratch_shapes=[pltpu.VMEM((GROUP, GROUP), F32), pltpu.VMEM((GROUP, GROUP), F32)],
        compiler_params=pltpu.CompilerParams(vmem_limit_bytes=16 * MIB),
        cost_estimate=pl.CostEstimate(
            flops=20_000_000_000, bytes_accessed=8 * MIB, transcendentals=blocks * heads * GROUP * GROUP
        ),
    )(activation, upstream, write_vectors, read_vectors, tables, tables, tables, tables)

    carried = pl.pallas_call(
        partial(scan_kernel, piece_rows),
        name="scan",
        in_specs=[vmem, pl.BlockSpec(memory_space=pltpu.HBM)],
        out_specs=vmem,
        out_shape=jax.ShapeDtypeStruct((count, 2 * piece_rows, LANES), F32),
        compiler_params=pltpu.CompilerParams(vmem_limit_bytes=8 * MIB),
    )(got, done)
    carried = lax.all_to_all(carried, "seq", 0, 0)

    act_grad, log_grad, write_grad, read_grad = pl.pallas_call(
        partial(cross_kernel, heads, piece_rows),
        name="cross",
        in_specs=[vmem] * 13,
        out_specs=[hbm] + [vmem] * 3,
        out_shape=[low, across, part, part],
        scratch_shapes=[pltpu.VMEM((rows, inner), BF16), pltpu.SemaphoreType.DMA((bunches,))],
        compiler_params=pltpu.CompilerParams(vmem_limit_bytes=16 * MIB),
        cost_estimate=pl.CostEstimate(flops=8 * rows * state * inner, bytes_accessed=16 * MIB, transcendentals=0),
    )(
        act_scaled, up_scaled, back, carried, inside, tables, spread, local_rows, local_columns,
        write_vectors, read_vectors, write_part, read_part,
    )
    return act_grad, log_grad.T, write_grad, read_grad


def solution(mesh):
    spread = P(("dp", "seq"), None)
    return jax.shard_map(
        on_device,
        mesh=mesh,
        in_specs=(spread, spread, P("dp"), spread, spread, spread),
        out_specs=(spread, spread, spread, spread),
        check_vma=False,
    )
```

time: 127 us -> 95.5 us (0.75)
  local copies, waits for them, and re-layouts: 28.8 us -> 9.27 us
  blocking collectives: 44.4 us -> 34.5 us
  waiting for transfers between devices: 13.4 us -> 5.83 us
  starting transfers between devices: 5.89 us -> 11.6 us
    unnamed x57 -> x32, local copies, waits for them, and re-layouts: 27.1 us -> 9.27 us
    pallas_call x1, Pallas kernels: 8.35 us -> 18.3 us  [on_device(): pl.pallas_call(local_kernel, name='local', grid=(blocks, bunches), in_spe...]
    all_to_all x1, blocking collectives: 44.4 us -> 34.5 us  [on_device(): carried = lax.all_to_all(carried, 'seq', 0, 0)]
    pallas_call x1, Pallas kernels: 15.1 us -> 7.14 us  [on_device(): pl.pallas_call(partial(cross_kernel, heads, piece_rows), name='cross', in...]
    all_to_all x1, waiting for transfers between devices: 13.4 us -> 5.83 us  [on_device(): got = lax.all_to_all(pieces, 'seq', 0, 0)]
    all_to_all x1, starting transfers between devices: 5.89 us -> 11.6 us  [on_device(): got = lax.all_to_all(pieces, 'seq', 0, 0)]
    pallas_call x1 -> x0, local copies, waits for them, and re-layouts: 1.69 us -> none  [on_device(): pl.pallas_call(partial(cross_kernel, heads, piece_rows), name='cross', gr...]
    pallas_call x1, Pallas kernels: 8.9 us -> 7.38 us  [on_device(): pl.pallas_call(partial(states_kernel, heads, piece_rows), name='states',...]
  transfers between devices with their start and end apart: 1 -> 1, of which waited for: 1 -> 1; matrix products, arithmetic and copies ran while one was open for 0% -> 0% of each run, Pallas kernels for 7% -> 19%
where the time goes in v2:
time: 95.5 us; the launch traced here: 95.2 us
  blocking collectives  34.5 us (36%)
  Pallas kernels  33.1 us (35%)
  starting transfers between devices  11.6 us (12%)
  local copies, waits for them, and re-layouts  9.27 us (10%)
  waiting for transfers between devices  5.83 us (6%)
    all_to_all x1, blocking collectives, on_device(): carried = lax.all_to_all(carried, 'seq', 0, 0)  34.5 us
    pallas_call x1, Pallas kernels, on_device(): pl.pallas_call(local_kernel, name='local', grid=(blocks, bunches), in_spe...  18.3 us
    all_to_all x1, starting transfers between devices, on_device(): got = lax.all_to_all(pieces, 'seq', 0, 0)  11.6 us
    unnamed x32, local copies, waits for them, and re-layouts  9.27 us
    pallas_call x1, Pallas kernels, on_device(): pl.pallas_call(partial(states_kernel, heads, piece_rows), name='states',...  7.38 us
    pallas_call x1, Pallas kernels, on_device(): pl.pallas_call(partial(cross_kernel, heads, piece_rows), name='cross', in...  7.14 us
    all_to_all x1, waiting for transfers between devices, on_device(): got = lax.all_to_all(pieces, 'seq', 0, 0)  5.83 us
  transfers between devices with their start and end apart: 1, of which 1 were waited for; matrix products, arithmetic and copies ran while one was open for 0% of the time, Pallas kernels for 19%

profile of v2, /device:TPU:0, one launch (start us, length us, event | category | flops | bytes accessed | tf_op | source)
XLA Modules:
  0.0 95.2 jit_solution(14718916019039759110)
XLA Ops:
  0.6 7.4 %states.1 = (f32[64,72,128]{2,1,0:T(8,128)}, f32[160,512]{1,0:T(8,128)}, f32[8,2048]{1,0:T(8,128)}) custom-call(f32[32,512]{1,0:T(8,128)} %bitcast.3, f32[1,32]{1,0:T(1,128)} %bitcast.4, bf16[512,128]{1,0:T(8,128)(2,1)} %write_ref.5, bf16[512,128]{1,0:T(8,128)(2,1)} %read_ref.5, bf16[512,2048]{1,0:T(8,128)(2,1)} %act_ref.3, bf16[512,2048]{1,0:T(8,128)(2,1)} %up_ref.3), custom_call_target="tpu_custom_call" | custom-call | flops 536870912 | bytes 8388608 | tf_op jit(solution)/shard_map/states/pallas_call | solution.py:382
  8.0 0.0 copy-start.10
  8.0 0.0 copy-start.11
  8.0 0.0 copy-start.12
  8.1 11.6 %all-to-all-start = ((f32[64,72,128]{2,1,0:T(8,128)}), f32[64,72,128]{2,1,0:T(8,128)S(1)}, u32[]{:S(2)}, u32[]{:S(2)}) async-start(f32[64,72,128]{2,1,0:T(8,128)} %get-tuple-element.24), calls=%async_computation | async-start | bytes 4718592 | tf_op jit(solution)/shard_map/all_to_all | solution.py:409
  19.7 0.0 copy-done.10
  19.7 0.0 copy-done.11
  19.7 0.0 copy-done.12
  19.7 0.0 copy-start
  19.8 1.6 %copy-done = bf16[512,2048]{1,0:T(8,128)(2,1)S(1)} copy-done((bf16[512,2048]{1,0:T(8,128)(2,1)S(1)}, bf16[512,2048]{1,0:T(8,128)(2,1)}, u32[]{:S(2)}) %copy-start) | copy-done | bytes 2097176
  21.3 0.0 copy-start.1
  21.3 1.6 %copy-done.1 = bf16[512,2048]{1,0:T(8,128)(2,1)S(1)} copy-done((bf16[512,2048]{1,0:T(8,128)(2,1)S(1)}, bf16[512,2048]{1,0:T(8,128)(2,1)}, u32[]{:S(2)}) %copy-start.1) | copy-done | bytes 2097176
  22.9 18.3 %local.1 = (bf16[512,2048]{1,0:T(8,128)(2,1)S(1)}, bf16[512,2048]{1,0:T(8,128)(2,1)S(1)}, bf16[512,2048]{1,0:T(8,128)(2,1)S(1)}, f32[2,128,2048]{2,1,0:T(8,128)S...) custom-call(bf16[512,2048]{1,0:T(8,128)(2,1)S(1)} %copy-done, ...), custom_call_target="tpu_custom_call" | custom-call | flops 20000000000 | bytes 8388608 | tf_op jit(solution)/shard_map/local/pallas_call | solution.py:417
  41.3 0.0 copy-start.2
  41.3 1.3 %copy-done.2 = bf16[512,2048]{1,0:T(8,128)(2,1)} copy-done((bf16[512,2048]{1,0:T(8,128)(2,1)}, bf16[512,2048]{1,0:T(8,128)(2,1)S(1)}, u32[]{:S(2)}) %copy-start.2) | copy-done | bytes 2097176
  42.6 0.0 copy-start.4
  42.6 1.3 %copy-done.4 = bf16[512,2048]{1,0:T(8,128)(2,1)} copy-done((bf16[512,2048]{1,0:T(8,128)(2,1)}, bf16[512,2048]{1,0:T(8,128)(2,1)S(1)}, u32[]{:S(2)}) %copy-start.4) | copy-done | bytes 2097176
  43.9 0.0 copy-start.6
  43.9 1.4 %copy-done.6 = bf16[512,2048]{1,0:T(8,128)(2,1)} copy-done((bf16[512,2048]{1,0:T(8,128)(2,1)}, bf16[512,2048]{1,0:T(8,128)(2,1)S(1)}, u32[]{:S(2)}) %copy-start.6) | copy-done | bytes 2097176
  45.3 0.0 copy-start.8
  45.3 1.4 %copy-done.8 = f32[2,128,2048]{2,1,0:T(8,128)} copy-done((f32[2,128,2048]{2,1,0:T(8,128)}, f32[2,128,2048]{2,1,0:T(8,128)S(1)}, u32[]{:S(2)}) %copy-start.8) | copy-done | bytes 2097176
  46.7 0.0 copy-start.14
  46.7 0.6 copy-done.14
  47.3 5.8 %all-to-all-done.got_ref = f32[64,72,128]{2,1,0:T(8,128)S(1)} async-done(((f32[64,72,128]{2,1,0:T(8,128)}), f32[64,72,128]{2,1,0:T(8,128)S(1)}, u32[]{:S(2)}, u32[]{:S(2)}) %all-to-all-start) | async-done | bytes 2359328 | tf_op jit(solution)/shard_map/all_to_all | solution.py:409
  53.2 0.0 copy-start.7
  53.2 0.0 copy-start.9
  53.2 0.0 copy-start.13
  53.2 0.0 copy-start.15
  53.2 0.3 scan.1
  53.4 0.0 copy-start.3
  53.4 0.0 copy-start.5
  53.5 34.5 %all_to_all.10.carried_ref = f32[64,64,128]{2,1,0:T(8,128)S(1)} all-to-all(f32[64,64,128]{2,1,0:T(8,128)S(1)} %scan.1), channel_id=1, replica_groups=mesh['seq'=64,'dp'=2] {'seq'}, dimensions={0} | all-to-all | bytes 4194304 | tf_op jit(solution)/shard_map/all_to_all | solution.py:449
  88.0 0.0 copy-done.7
  88.0 0.0 copy-done.9
  88.0 0.0 copy-done.13
  88.0 0.0 copy-done.15
  88.0 0.0 copy-done.3
  88.0 0.0 copy-done.5
  88.0 7.1 %cross.1 = (bf16[512,2048]{1,0:T(8,128)(2,1)}, f32[32,512]{1,0:T(8,128)}, f32[512,128]{1,0:T(8,128)}, f32[512,128]{1,0:T(8,128)}) custom-call(bf16[512,2048]{1,0:T(8,128)(2,1)S(1)} %copy-done.5, bf16[512,2048]{1,0:T(8,128)(2,1)S(1)} %copy-done.7, bf16[512,2048]{1,0:T(8,128)(2,1)S(1)} %copy-done.3, f32[64,64,128]{2,1,0:T(8,128)S(1)} %all_to_all.10.carried_ref, ...), custom_call_target="tpu_custom_call" | custom-call | flops 1073741824 | bytes 16777216 | tf_op jit(solution)/shard_map/cross/pallas_call | solution.py:451
Async XLA Ops:
  8.0 11.7 %copy-start.10 = (bf16[512,128]{1,0:T(8,128)(2,1)S(1)}, bf16[512,128]{1,0:T(8,128)(2,1)}, u32[]{:S(2)}) copy-start(bf16[512,128]{1,0:T(8,128)(2,1)} %write_ref.5) | copy-start | bytes 393220
  8.0 11.7 %copy-start.11 = (bf16[512,128]{1,0:T(8,128)(2,1)S(1)}, bf16[512,128]{1,0:T(8,128)(2,1)}, u32[]{:S(2)}) copy-start(bf16[512,128]{1,0:T(8,128)(2,1)} %read_ref.5) | copy-start | bytes 393220
  8.0 11.7 %copy-start.12 = (f32[160,512]{1,0:T(8,128)S(1)}, f32[160,512]{1,0:T(8,128)}, u32[]{:S(2)}) copy-start(f32[160,512]{1,0:T(8,128)} %get-tuple-element.20.running_ref.shifted_ref.out_ref.in_ref.tables_ref) | copy-start | bytes 983044
  8.1 45.1 %all-to-all-start = ((f32[64,72,128]{2,1,0:T(8,128)}), f32[64,72,128]{2,1,0:T(8,128)S(1)}, u32[]{:S(2)}, u32[]{:S(2)}) async-start(f32[64,72,128]{2,1,0:T(8,128)} %get-tuple-element.24), calls=%async_computation | async-start | bytes 4718592 | tf_op jit(solution)/shard_map/all_to_all | solution.py:409
  19.7 1.6 %copy-start = (bf16[512,2048]{1,0:T(8,128)(2,1)S(1)}, bf16[512,2048]{1,0:T(8,128)(2,1)}, u32[]{:S(2)}) copy-start(bf16[512,2048]{1,0:T(8,128)(2,1)} %act_ref.3) | copy-start | bytes 6291460
  21.3 1.6 %copy-start.1 = (bf16[512,2048]{1,0:T(8,128)(2,1)S(1)}, bf16[512,2048]{1,0:T(8,128)(2,1)}, u32[]{:S(2)}) copy-start(bf16[512,2048]{1,0:T(8,128)(2,1)} %up_ref.3) | copy-start | bytes 6291460
  41.3 1.3 %copy-start.2 = (bf16[512,2048]{1,0:T(8,128)(2,1)}, bf16[512,2048]{1,0:T(8,128)(2,1)S(1)}, u32[]{:S(2)}) copy-start(bf16[512,2048]{1,0:T(8,128)(2,1)S(1)} %get-tuple-element.23.back_ref) | copy-start | bytes 6291460
  42.6 1.3 %copy-start.4 = (bf16[512,2048]{1,0:T(8,128)(2,1)}, bf16[512,2048]{1,0:T(8,128)(2,1)S(1)}, u32[]{:S(2)}) copy-start(bf16[512,2048]{1,0:T(8,128)(2,1)S(1)} %get-tuple-element.21.act_scaled_ref) | copy-start | bytes 6291460
  43.9 1.4 %copy-start.6 = (bf16[512,2048]{1,0:T(8,128)(2,1)}, bf16[512,2048]{1,0:T(8,128)(2,1)S(1)}, u32[]{:S(2)}) copy-start(bf16[512,2048]{1,0:T(8,128)(2,1)S(1)} %get-tuple-element.22.up_scaled_ref) | copy-start | bytes 6291460
  45.3 1.4 %copy-start.8 = (f32[2,128,2048]{2,1,0:T(8,128)}, f32[2,128,2048]{2,1,0:T(8,128)S(1)}, u32[]{:S(2)}) copy-start(f32[2,128,2048]{2,1,0:T(8,128)S(1)} %get-tuple-element.26.inside_ref) | copy-start | bytes 6291460
  46.7 0.6 copy-start.14
  53.2 34.8 %copy-start.7 = (bf16[512,2048]{1,0:T(8,128)(2,1)S(1)}, bf16[512,2048]{1,0:T(8,128)(2,1)}, u32[]{:S(2)}) copy-start(bf16[512,2048]{1,0:T(8,128)(2,1)} %copy-done.6) | copy-start | bytes 6291460
  53.2 34.8 %copy-start.9 = (f32[2,128,2048]{2,1,0:T(8,128)S(1)}, f32[2,128,2048]{2,1,0:T(8,128)}, u32[]{:S(2)}) copy-start(f32[2,128,2048]{2,1,0:T(8,128)} %copy-done.8) | copy-start | bytes 6291460
  53.2 34.8 %copy-start.13 = (f32[8,2048]{1,0:T(8,128)S(1)}, f32[8,2048]{1,0:T(8,128)}, u32[]{:S(2)}) copy-start(f32[8,2048]{1,0:T(8,128)} %get-tuple-element.27.spread_ref) | copy-start | bytes 196612
  53.2 34.9 %copy-start.15 = (f32[32,512]{1,0:T(8,128)S(1)}, f32[32,512]{1,0:T(8,128)}, u32[]{:S(2)}) copy-start(f32[32,512]{1,0:T(8,128)} %copy-done.14) | copy-start | bytes 196612
  53.4 34.6 %copy-start.3 = (bf16[512,2048]{1,0:T(8,128)(2,1)S(1)}, bf16[512,2048]{1,0:T(8,128)(2,1)}, u32[]{:S(2)}) copy-start(bf16[512,2048]{1,0:T(8,128)(2,1)} %copy-done.2) | copy-start | bytes 6291460
  53.4 34.6 %copy-start.5 = (bf16[512,2048]{1,0:T(8,128)(2,1)S(1)}, bf16[512,2048]{1,0:T(8,128)(2,1)}, u32[]{:S(2)}) copy-start(bf16[512,2048]{1,0:T(8,128)(2,1)} %copy-done.4) | copy-start | bytes 6291460

commit v3 on v2

--- a/solution.py
+++ b/solution.py
@@ -195,12 +195,13 @@
 
 def local_kernel(
     act_ref, up_ref, write_ref, read_ref, running_ref, shifted_ref, out_ref, in_ref,
-    back_ref, act_scaled_ref, up_scaled_ref, inside_ref, rows_ref, columns_ref, write_part_ref, read_part_ref, done_ref,
+    back_ref, act_scaled_ref, up_scaled_ref, inside_ref, write_part_ref, read_part_ref, done_ref,
     pair_sum, scores,
 ):
     bunch = pl.program_id(1)
     half = GROUP // 2
     wide = act_ref.shape[1]
+    state = write_ref.shape[1]
     triangle = lax.broadcasted_iota(jnp.int32, (half, half), 0) <= lax.broadcasted_iota(
         jnp.int32, (half, half), 1
     )
@@ -213,16 +214,16 @@
     table = channel_table(BUNCH, wide).astype(BF16)
     act_scaled = (act_ref[...].astype(F32) * spread_heads(out_ref[...], table)).astype(BF16)
     up_scaled = (up_ref[...].astype(F32) * spread_heads(in_ref[...], table)).astype(BF16)
-    act_scaled_ref[...] = act_scaled
-    up_scaled_ref[...] = up_scaled
+    act_scaled_ref[...] = act_scaled.T
+    up_scaled_ref[...] = up_scaled.T
 
     @pl.when(pl.program_id(0) == 0)
     def _():
-        inside_ref[0] = dot_tn(write_ref[...], act_scaled)
+        inside_ref[0, :state, :] = dot_tn(write_ref[...], act_scaled)
 
     @pl.when(pl.program_id(0) == 1)
     def _():
-        inside_ref[0] = dot_tn(read_ref[...], up_scaled)
+        inside_ref[0, :state, :] = dot_tn(read_ref[...], up_scaled)
 
     shifted = jnp.concatenate([shifted_ref[...], jnp.zeros((LANES - BUNCH, GROUP), F32)], axis=0).T
     left = left_half(GROUP)
@@ -253,8 +254,8 @@
             masked_low = (decay_c * scores[half:, half:]).astype(BF16)
             sums = jnp.sum(masked_top.astype(F32) * dots_top, axis=0, keepdims=True)
             low_sums = jnp.sum(masked_low.astype(F32) * dots_low, axis=0, keepdims=True)
-            rows_ref[head : head + 1, :half] = sums[:, :half]
-            rows_ref[head : head + 1, half:] = sums[:, half:] + low_sums
+            inside_ref[0, state + head : state + head + 1, :half] = sums[:, :half]
+            inside_ref[0, state + head : state + head + 1, half:GROUP] = sums[:, half:] + low_sums
             back_top += dot_nn(masked_top, up_one)
             back_low += dot_nn(masked_low, up_one[half:])
         back = jnp.concatenate([back_top, back_low], axis=0)
@@ -264,7 +265,7 @@
             keep = left if side == 0 else jnp.logical_not(left)
             one = jnp.sum(jnp.where(keep, product, 0.0), axis=1, keepdims=True)
             columns = jnp.where(lane == 2 * pair + side, one, columns)
-    columns_ref[...] = columns.T[:BUNCH]
+    inside_ref[0, state + BUNCH :, :GROUP] = columns.T[:BUNCH]
 
     @pl.when(bunch == pl.num_programs(1) - 1)
     def _():
@@ -274,19 +275,22 @@
         read_part_ref[...] = dot_tn(low, write_ref[...])
 
 
-def halves(value):
-    high = value.astype(BF16)
-    return [high, (value - high.astype(F32)).astype(BF16)]
-
-
 def cross_kernel(
     heads, piece_rows, act_scaled_ref, up_scaled_ref, back_ref, carried_ref, inside_ref, tables_ref, spread_ref,
-    rows_ref, columns_ref, write_ref, read_ref, write_part_ref, read_part_ref,
-    act_grad_ref, log_ref, write_grad_ref, read_grad_ref, act_grad_buf, sems,
+    write_ref, read_ref, write_part_ref, read_part_ref,
+    act_grad_ref, log_ref, write_grad_ref, read_grad_ref, act_grad_buf, read_acc, write_acc, read_buf, write_buf, sems, part_sems,
 ):
-    rows, inner = act_scaled_ref.shape
+    inner, rows = act_scaled_ref.shape
     blocks = rows // GROUP
     bunches = heads // BUNCH
+    channels = inner // heads
+    state = write_ref.shape[1]
+    parts = [
+        pltpu.make_async_copy(source, target, part_sems.at[which])
+        for which, (source, target) in enumerate(((write_part_ref, write_buf), (read_part_ref, read_buf)))
+    ]
+    for copy in parts:
+        copy.start()
     wide = inner // bunches
     per_pair = LANES // piece_rows
 
@@ -303,20 +307,31 @@
 
     table = channel_table(BUNCH, wide)
     table_low = table.astype(BF16)
-    channel = lax.broadcasted_iota(jnp.int32, (2 * BUNCH, 4 * wide), 1)
-    lane = lax.broadcasted_iota(jnp.int32, (2 * BUNCH, 4 * wide), 0)
-    place = channel // (2 * wide) * BUNCH + channel % wide // (wide // BUNCH)
-    gather_table = jnp.where(lane == place, 1.0, 0.0).astype(BF16)
+    write_across = [write_ref[b * GROUP : (b + 1) * GROUP, :].T for b in range(blocks)]
+    read_across = [read_ref[b * GROUP : (b + 1) * GROUP, :].T for b in range(blocks)]
+
+    def head_sums(product):
+        return jnp.concatenate(
+            [
+                jnp.sum(product[h * channels : (h + 1) * channels], axis=0, keepdims=True)
+                for h in range(BUNCH)
+            ],
+            axis=0,
+        )
+
     order = order_table(GROUP, False)
     copies = []
     for bunch in range(bunches):
+        if bunch == bunches - 1:
+            for copy in parts:
+                copy.wait()
         lanes = slice(bunch * wide, (bunch + 1) * wide)
         some = slice(bunch * BUNCH, (bunch + 1) * BUNCH)
         first, second = spread_ref[0:1, lanes], spread_ref[1:2, lanes]
         enter_0, leave_1 = gather(0, bunch), gather(piece_rows, bunch)
         kept_0, kept_1 = first * enter_0, second * leave_1
-        enter_1 = kept_0 + inside_ref[0, :, lanes]
-        leave_0 = inside_ref[1, :, lanes] + kept_1
+        enter_1 = kept_0 + inside_ref[0, :state, lanes]
+        leave_0 = inside_ref[1, :state, lanes] + kept_1
         enters, leaves = (enter_0, enter_1), (leave_0, leave_1)
         edges = [
             jnp.sum(table * jnp.sum(product, axis=0, keepdims=True), axis=1, keepdims=True)
@@ -327,28 +342,28 @@
             span = slice(block * GROUP, (block + 1) * GROUP)
             enter_low = enters[block].astype(BF16)
             leave_low = leaves[block].astype(BF16)
-            offset = dot_nn(read_ref[span, :], enter_low)
             cross = dot_nn(write_ref[span, :], leave_low)
             decay_out = spread_heads(tables_ref[2 * heads + bunch * BUNCH : 2 * heads + (bunch + 1) * BUNCH, span], table_low)
             act_grad_buf[span, lanes] = (back_ref[span, lanes].astype(F32) + decay_out * cross).astype(BF16)
-            act_scaled, up_scaled = act_scaled_ref[span, lanes], up_scaled_ref[span, lanes]
-            row_products = offset * up_scaled.astype(F32)
-            col_products = cross * act_scaled.astype(F32)
-            sums = dot_nt(
-                gather_table, jnp.concatenate(halves(row_products) + halves(col_products), axis=1)
-            )
-            column = columns_ref[some, span] + sums[BUNCH:]
-            nets.append(rows_ref[some, span] + sums[:BUNCH] - column)
+            act_scaled, up_scaled = act_scaled_ref[lanes, span], up_scaled_ref[lanes, span]
+            row_sums = head_sums(dot_tn(enter_low, read_across[block]) * up_scaled.astype(F32))
+            col_sums = head_sums(dot_tn(leave_low, write_across[block]) * act_scaled.astype(F32))
+            near = slice(bunch * wide, bunch * wide + GROUP)
+            column = inside_ref[block, state + BUNCH :, near] + col_sums
+            nets.append(inside_ref[block, state : state + BUNCH, near] + row_sums - column)
             cols.append(column)
-            edges[block] += jnp.sum(sums[BUNCH:], axis=1, keepdims=True)
-            read_cross = dot_nt(up_scaled, enter_low)
-            write_cross = dot_nt(act_scaled, leave_low)
+            edges[block] += jnp.sum(col_sums, axis=1, keepdims=True)
+            read_cross = dot_nn(enter_low, up_scaled)
+            write_cross = dot_nn(leave_low, act_scaled)
             if bunch == 0:
-                read_grad_ref[span, :] = read_part_ref[span, :] + read_cross
-                write_grad_ref[span, :] = write_part_ref[span, :] + write_cross
+                read_acc[:, span] = read_cross
+                write_acc[:, span] = write_cross
+            elif bunch < bunches - 1:
+                read_acc[:, span] += read_cross
+                write_acc[:, span] += write_cross
             else:
-                read_grad_ref[span, :] += read_cross
-                write_grad_ref[span, :] += write_cross
+                read_buf[span, :] += (read_acc[:, span] + read_cross).T
+                write_buf[span, :] += (write_acc[:, span] + write_cross).T
         few = pl.ds(bunch * wide, wide)
         copy = pltpu.make_async_copy(act_grad_buf.at[:, few], act_grad_ref.at[:, few], sems.at[bunch])
         copy.start()
@@ -358,6 +373,10 @@
             span = slice(block * GROUP, (block + 1) * GROUP)
             log_grad = suffix[block * BUNCH : (block + 1) * BUNCH] + edges[block]
             log_ref[some, span] = cols[block] + tables_ref[4 * heads + bunch * BUNCH : 4 * heads + (bunch + 1) * BUNCH, span] * log_grad
+    for which, (source, target) in enumerate(((write_buf, write_grad_ref), (read_buf, read_grad_ref))):
+        copy = pltpu.make_async_copy(source, target, part_sems.at[2 + which])
+        copy.start()
+        copies.append(copy)
     for copy in copies:
         copy.wait()
 
@@ -377,6 +396,7 @@
     hbm = pl.BlockSpec(memory_space=pl.ANY)
     across = jax.ShapeDtypeStruct((heads, rows), F32)
     low = jax.ShapeDtypeStruct((rows, inner), BF16)
+    low_across = jax.ShapeDtypeStruct((inner, rows), BF16)
     part = jax.ShapeDtypeStruct((rows, state), F32)
 
     pieces, tables, spread = pl.pallas_call(
@@ -408,31 +428,29 @@
 
     got = lax.all_to_all(pieces, "seq", 0, 0)
 
-    narrow = pl.BlockSpec((BUNCH, GROUP), lambda b, g: (g, b))
     def table(which):
         return pl.BlockSpec((BUNCH, GROUP), lambda b, g: (which * bunches + g, b))
 
     block_wide = pl.BlockSpec((GROUP, wide), lambda b, g: (b, g))
+    block_tall = pl.BlockSpec((wide, GROUP), lambda b, g: (g, b))
     block_state = pl.BlockSpec((GROUP, state), lambda b, g: (b, 0))
-    back, act_scaled, up_scaled, inside, local_rows, local_columns, write_part, read_part, done = pl.pallas_call(
+    back, act_scaled, up_scaled, inside, write_part, read_part, done = pl.pallas_call(
         local_kernel,
         name="local",
         grid=(blocks, bunches),
         in_specs=[block_wide, block_wide, block_state, block_state] + [table(i) for i in range(4)],
         out_specs=[
             block_wide,
-            block_wide,
-            block_wide,
-            pl.BlockSpec((1, state, wide), lambda b, g: (b, 0, g)),
-            narrow,
-            narrow,
+            block_tall,
+            block_tall,
+            pl.BlockSpec((1, state + 2 * BUNCH, wide), lambda b, g: (b, 0, g)),
             block_state,
             block_state,
             pl.BlockSpec((8, LANES), lambda b, g: (0, 0)),
         ],
-        out_shape=[low, low, low, jax.ShapeDtypeStruct((blocks, state, inner), F32), across, across, part, part, jax.ShapeDtypeStruct((8, LANES), F32)],
+        out_shape=[low, low_across, low_across, jax.ShapeDtypeStruct((blocks, state + 2 * BUNCH, inner), F32), part, part, jax.ShapeDtypeStruct((8, LANES), F32)],
         scratch_shapes=[pltpu.VMEM((GROUP, GROUP), F32), pltpu.VMEM((GROUP, GROUP), F32)],
-        compiler_params=pltpu.CompilerParams(vmem_limit_bytes=16 * MIB),
+        compiler_params=pltpu.CompilerParams(vmem_limit_bytes=56 * MIB),
         cost_estimate=pl.CostEstimate(
             flops=20_000_000_000, bytes_accessed=8 * MIB, transcendentals=blocks * heads * GROUP * GROUP
         ),
@@ -451,14 +469,23 @@
     act_grad, log_grad, write_grad, read_grad = pl.pallas_call(
         partial(cross_kernel, heads, piece_rows),
         name="cross",
-        in_specs=[vmem] * 13,
-        out_specs=[hbm] + [vmem] * 3,
+        in_specs=[vmem] * 9 + [hbm] * 2,
+        out_specs=[hbm, vmem, hbm, hbm],
+        input_output_aliases={9: 2, 10: 3},
         out_shape=[low, across, part, part],
-        scratch_shapes=[pltpu.VMEM((rows, inner), BF16), pltpu.SemaphoreType.DMA((bunches,))],
+        scratch_shapes=[
+            pltpu.VMEM((rows, inner), BF16),
+            pltpu.VMEM((state, rows), F32),
+            pltpu.VMEM((state, rows), F32),
+            pltpu.VMEM((rows, state), F32),
+            pltpu.VMEM((rows, state), F32),
+            pltpu.SemaphoreType.DMA((bunches,)),
+            pltpu.SemaphoreType.DMA((4,)),
+        ],
         compiler_params=pltpu.CompilerParams(vmem_limit_bytes=16 * MIB),
         cost_estimate=pl.CostEstimate(flops=8 * rows * state * inner, bytes_accessed=16 * MIB, transcendentals=0),
     )(
-        act_scaled, up_scaled, back, carried, inside, tables, spread, local_rows, local_columns,
+        act_scaled, up_scaled, back, carried, inside, tables, spread,
         write_vectors, read_vectors, write_part, read_part,
     )
     return act_grad, log_grad.T, write_grad, read_grad

time: 95.5 us -> 94.1 us (0.985)
  local copies, waits for them, and re-layouts: 9.27 us -> 0.71 us
  waiting for transfers between devices: 5.83 us -> 12.6 us
    unnamed x32 -> x18, local copies, waits for them, and re-layouts: 9.27 us -> 0.71 us
    all_to_all x1, waiting for transfers between devices: 5.83 us -> 12.6 us  [on_device(): got = lax.all_to_all(pieces, 'seq', 0, 0)]
    pallas_call x1, Pallas kernels: 18.3 us -> 20.8 us  [on_device(): pl.pallas_call(local_kernel, name='local', grid=(blocks, bunches), in_spe...]
    pallas_call x1, Pallas kernels: 7.14 us -> 5.23 us  [on_device(): pl.pallas_call(partial(cross_kernel, heads, piece_rows), name='cross', in...]
  transfers between devices with their start and end apart: 1 -> 1, of which waited for: 1 -> 1; matrix products, arithmetic and copies ran while one was open for 0% -> 0% of each run, Pallas kernels for 19% -> 22%
where the time goes in v3:
time: 94.1 us; the launch traced here: 93.8 us
  blocking collectives  34.5 us (37%)
  Pallas kernels  33.6 us (36%)
  waiting for transfers between devices  12.6 us (13%)
  starting transfers between devices  11.5 us (12%)
    all_to_all x1, blocking collectives, on_device(): carried = lax.all_to_all(carried, 'seq', 0, 0)  34.5 us
    pallas_call x1, Pallas kernels, on_device(): pl.pallas_call(local_kernel, name='local', grid=(blocks, bunches), in_spe...  20.8 us
    all_to_all x1, waiting for transfers between devices, on_device(): got = lax.all_to_all(pieces, 'seq', 0, 0)  12.6 us
    all_to_all x1, starting transfers between devices, on_device(): got = lax.all_to_all(pieces, 'seq', 0, 0)  11.5 us
    pallas_call x1, Pallas kernels, on_device(): pl.pallas_call(partial(states_kernel, heads, piece_rows), name='states',...  7.38 us
    pallas_call x1, Pallas kernels, on_device(): pl.pallas_call(partial(cross_kernel, heads, piece_rows), name='cross', in...  5.23 us
  transfers between devices with their start and end apart: 1, of which 1 were waited for; matrix products, arithmetic and copies ran while one was open for 0% of the time, Pallas kernels for 22%

profile of v3, /device:TPU:0, one launch (start us, length us, event | category | flops | bytes accessed | tf_op | source)
XLA Modules:
  0.0 93.8 jit_solution(3377904459724455371)
XLA Ops:
  0.6 7.4 %states.1 = (f32[64,72,128]{2,1,0:T(8,128)}, f32[160,512]{1,0:T(8,128)}, f32[8,2048]{1,0:T(8,128)}) custom-call(f32[32,512]{1,0:T(8,128)} %bitcast.3, f32[1,32]{1,0:T(1,128)} %bitcast.4, bf16[512,128]{1,0:T(8,128)(2,1)} %write_ref.5, bf16[512,128]{1,0:T(8,128)(2,1)} %read_ref.5, bf16[512,2048]{1,0:T(8,128)(2,1)} %act_ref.3, bf16[512,2048]{1,0:T(8,128)(2,1)} %up_ref.3), custom_call_target="tpu_custom_call" | custom-call | flops 536870912 | bytes 8388608 | tf_op jit(solution)/shard_map/states/pallas_call | solution.py:402
  8.0 11.5 %all-to-all-start = ((f32[64,72,128]{2,1,0:T(8,128)}), f32[64,72,128]{2,1,0:T(8,128)S(1)}, u32[]{:S(2)}, u32[]{:S(2)}) async-start(f32[64,72,128]{2,1,0:T(8,128)} %get-tuple-element.22), calls=%async_computation | async-start | bytes 4718592 | tf_op jit(solution)/shard_map/all_to_all | solution.py:429
  19.6 0.0 copy-start.4
  19.6 0.0 copy-start.5
  19.6 0.0 copy-start.6
  19.6 0.0 copy-start.7
  19.6 20.8 %local.1 = (bf16[512,2048]{1,0:T(8,128)(2,1)}, bf16[2048,512]{1,0:T(8,128)(2,1)}, bf16[2048,512]{1,0:T(8,128)(2,1)}, f32[2,144,2048]{2,1,0:T(8,128)}, f32[512,12...) custom-call(bf16[512,2048]{1,0:T(8,128)(2,1)} %act_ref.3, bf16[512,2048]{1,0:T(8,128)(2,1)} %up_ref.3, ...), custom_call_target="tpu_custom_call" | custom-call | flops 20000000000 | bytes 8388608 | tf_op jit(solution)/shard_map/local/pallas_call | solution.py:437
  40.4 12.6 %all-to-all-done.got_ref = f32[64,72,128]{2,1,0:T(8,128)S(1)} async-done(((f32[64,72,128]{2,1,0:T(8,128)}), f32[64,72,128]{2,1,0:T(8,128)S(1)}, u32[]{:S(2)}, u32[]{:S(2)}) %all-to-all-start) | async-done | bytes 2359328 | tf_op jit(solution)/shard_map/all_to_all | solution.py:429
  53.0 0.0 copy-start.8
  53.0 0.7 copy-done.8
  53.7 0.0 copy-start.1
  53.7 0.0 copy-start.2
  53.7 0.0 copy-start.3
  53.7 0.3 scan.1
  53.9 0.0 copy-start
  53.9 34.5 %all_to_all.10.carried_ref = f32[64,64,128]{2,1,0:T(8,128)S(1)} all-to-all(f32[64,64,128]{2,1,0:T(8,128)S(1)} %scan.1), channel_id=1, replica_groups=mesh['seq'=64,'dp'=2] {'seq'}, dimensions={0} | all-to-all | bytes 4194304 | tf_op jit(solution)/shard_map/all_to_all | solution.py:467
  88.5 0.0 copy-done.4
  88.5 0.0 copy-done.5
  88.5 0.0 copy-done.6
  88.5 0.0 copy-done.7
  88.5 0.0 copy-done.1
  88.5 0.0 copy-done.2
  88.5 0.0 copy-done.3
  88.5 0.0 copy-done
  88.5 5.2 %cross.1 = (bf16[512,2048]{1,0:T(8,128)(2,1)}, f32[32,512]{1,0:T(8,128)}, f32[512,128]{1,0:T(8,128)}, f32[512,128]{1,0:T(8,128)}) custom-call(bf16[2048,512]{1,0:T(8,128)(2,1)S(1)} %copy-done.2, bf16[2048,512]{1,0:T(8,128)(2,1)S(1)} %copy-done.3, bf16[512,2048]{1,0:T(8,128)(2,1)S(1)} %copy-done.1, ...), custom_call_target="tpu_custom_call", output_to_operand_aliasing={{2}: (9, {}), {3}: (10, {})} | custom-call | flops 1073741824 | bytes 16777216 | tf_op jit(solution)/shard_map/cross/pallas_call | solution.py:469
Async XLA Ops:
  8.0 45.0 %all-to-all-start = ((f32[64,72,128]{2,1,0:T(8,128)}), f32[64,72,128]{2,1,0:T(8,128)S(1)}, u32[]{:S(2)}, u32[]{:S(2)}) async-start(f32[64,72,128]{2,1,0:T(8,128)} %get-tuple-element.22), calls=%async_computation | async-start | bytes 4718592 | tf_op jit(solution)/shard_map/all_to_all | solution.py:429
  19.6 68.9 %copy-start.4 = (bf16[512,128]{1,0:T(8,128)(2,1)S(1)}, bf16[512,128]{1,0:T(8,128)(2,1)}, u32[]{:S(2)}) copy-start(bf16[512,128]{1,0:T(8,128)(2,1)} %write_ref.5) | copy-start | bytes 393220
  19.6 68.9 %copy-start.5 = (bf16[512,128]{1,0:T(8,128)(2,1)S(1)}, bf16[512,128]{1,0:T(8,128)(2,1)}, u32[]{:S(2)}) copy-start(bf16[512,128]{1,0:T(8,128)(2,1)} %read_ref.5) | copy-start | bytes 393220
  19.6 68.9 %copy-start.6 = (f32[160,512]{1,0:T(8,128)S(1)}, f32[160,512]{1,0:T(8,128)}, u32[]{:S(2)}) copy-start(f32[160,512]{1,0:T(8,128)} %get-tuple-element.18.running_ref.shifted_ref.out_ref.in_ref.tables_ref) | copy-start | bytes 983044
  19.6 68.9 %copy-start.7 = (f32[8,2048]{1,0:T(8,128)S(1)}, f32[8,2048]{1,0:T(8,128)}, u32[]{:S(2)}) copy-start(f32[8,2048]{1,0:T(8,128)} %get-tuple-element.25.spread_ref) | copy-start | bytes 196612
  53.0 0.7 copy-start.8
  53.7 34.8 %copy-start.1 = (bf16[512,2048]{1,0:T(8,128)(2,1)S(1)}, bf16[512,2048]{1,0:T(8,128)(2,1)}, u32[]{:S(2)}) copy-start(bf16[512,2048]{1,0:T(8,128)(2,1)} %get-tuple-element.21.back_ref) | copy-start | bytes 6291460
  53.7 34.8 %copy-start.2 = (bf16[2048,512]{1,0:T(8,128)(2,1)S(1)}, bf16[2048,512]{1,0:T(8,128)(2,1)}, u32[]{:S(2)}) copy-start(bf16[2048,512]{1,0:T(8,128)(2,1)} %get-tuple-element.19.act_scaled_ref) | copy-start | bytes 6291460
  53.7 34.8 %copy-start.3 = (bf16[2048,512]{1,0:T(8,128)(2,1)S(1)}, bf16[2048,512]{1,0:T(8,128)(2,1)}, u32[]{:S(2)}) copy-start(bf16[2048,512]{1,0:T(8,128)(2,1)} %get-tuple-element.20.up_scaled_ref) | copy-start | bytes 6291460
  53.9 34.6 %copy-start = (f32[2,144,2048]{2,1,0:T(8,128)S(1)}, f32[2,144,2048]{2,1,0:T(8,128)}, u32[]{:S(2)}) copy-start(f32[2,144,2048]{2,1,0:T(8,128)} %get-tuple-element.24.inside_ref) | copy-start | bytes 7077892

commit v4 on v3

--- a/solution.py
+++ b/solution.py
@@ -16,7 +16,8 @@
 BF16 = jnp.bfloat16
 MIB = 1 << 20
 VMEM_LIMIT = 56 * MIB
-AHEAD = 4
+AHEAD = 2
+STEP = 16
 
 
 def dot_nn(a, b):
@@ -73,8 +74,8 @@
 ):
     rows = dt_ref.shape[1]
     blocks = rows // GROUP
-    bunches = heads // BUNCH
-    wide = BUNCH // 2 * LANES
+    bunches = heads // STEP
+    wide = STEP // 2 * LANES
     small = [
         pltpu.make_async_copy(source, target, small_sems.at[which])
         for which, (source, target) in enumerate(
@@ -125,11 +126,11 @@
         [jnp.exp(device_total - first_running), leaving[heads:]], axis=1
     )
     columns = [jnp.exp(first_total), jnp.exp(second_total), jnp.exp(device_total)]
-    table = channel_table(BUNCH, wide)
+    table = channel_table(STEP, wide)
     table_low = table.astype(BF16)
     for bunch in range(bunches):
         lanes = slice(bunch * wide, (bunch + 1) * wide)
-        some = slice(bunch * BUNCH, (bunch + 1) * BUNCH)
+        some = slice(bunch * STEP, (bunch + 1) * STEP)
         first, second, both = (
             jnp.sum(table * column[some], axis=0, keepdims=True) for column in columns
         )
@@ -143,7 +144,7 @@
     stores = []
     for bunch in range(bunches):
         lanes = slice(bunch * wide, (bunch + 1) * wide)
-        some = slice(bunch * BUNCH, (bunch + 1) * BUNCH)
+        some = slice(bunch * STEP, (bunch + 1) * STEP)
         both = spread_ref[2:3, lanes]
         loads[2 * bunch].wait()
         if 2 * bunch + AHEAD < len(loads):
@@ -155,8 +156,8 @@
             loads[2 * bunch + 1 + AHEAD].start()
         up_scaled = up_buf[:, lanes].astype(F32) * spread_heads(device_in[some], table_low)
         grad = dot_nn(read_across, up_scaled.astype(BF16))
-        for local in range(BUNCH // 2):
-            pair = bunch * BUNCH // 2 + local
+        for local in range(STEP // 2):
+            pair = bunch * STEP // 2 + local
             here = slice(local * LANES, (local + 1) * LANES)
             few = slice(pair * per_pair, (pair + 1) * per_pair)
             piece_buf[few, :piece_rows, :] = state[:, here].reshape(per_pair, piece_rows, LANES)
@@ -166,7 +167,7 @@
             piece_buf[few, 2 * piece_rows :, :] = jnp.broadcast_to(
                 both[:, here][None], (per_pair, 8, LANES)
             )
-        few = pl.ds(bunch * BUNCH // 2 * per_pair, BUNCH // 2 * per_pair)
+        few = pl.ds(bunch * STEP // 2 * per_pair, STEP // 2 * per_pair)
         copy = pltpu.make_async_copy(piece_buf.at[few], pieces_ref.at[few], out_sems.at[bunch])
         copy.start()
         stores.append(copy)
@@ -418,9 +419,9 @@
             pltpu.VMEM((count, 2 * piece_rows + 8, LANES), F32),
             pltpu.VMEM((5 * heads, rows), F32),
             pltpu.VMEM((8, inner), F32),
-            pltpu.SemaphoreType.DMA((bunches, 2)),
+            pltpu.SemaphoreType.DMA((heads // STEP, 2)),
             pltpu.SemaphoreType.DMA((5,)),
-            pltpu.SemaphoreType.DMA((bunches,)),
+            pltpu.SemaphoreType.DMA((heads // STEP,)),
         ],
         compiler_params=pltpu.CompilerParams(vmem_limit_bytes=VMEM_LIMIT),
         cost_estimate=pl.CostEstimate(flops=4 * rows * state * inner, bytes_accessed=8 * MIB, transcendentals=0),

time: 94.1 us -> 92.8 us (0.986)
  Pallas kernels: 33.6 us -> 32.3 us
    pallas_call x1, Pallas kernels: 7.38 us -> 6.05 us  [on_device(): pl.pallas_call(partial(states_kernel, heads, piece_rows), name='states',...]
where the time goes in v4:
time: 92.8 us; the launch traced here: 92.4 us
  blocking collectives  34.6 us (37%)
  Pallas kernels  32.3 us (35%)
  waiting for transfers between devices  12.6 us (14%)
  starting transfers between devices  11.5 us (12%)
    all_to_all x1, blocking collectives, on_device(): carried = lax.all_to_all(carried, 'seq', 0, 0)  34.6 us
    pallas_call x1, Pallas kernels, on_device(): pl.pallas_call(local_kernel, name='local', grid=(blocks, bunches), in_spe...  20.8 us
    all_to_all x1, waiting for transfers between devices, on_device(): got = lax.all_to_all(pieces, 'seq', 0, 0)  12.6 us
    all_to_all x1, starting transfers between devices, on_device(): got = lax.all_to_all(pieces, 'seq', 0, 0)  11.5 us
    pallas_call x1, Pallas kernels, on_device(): pl.pallas_call(partial(states_kernel, heads, piece_rows), name='states',...  6.05 us
    pallas_call x1, Pallas kernels, on_device(): pl.pallas_call(partial(cross_kernel, heads, piece_rows), name='cross', in...  5.22 us
  transfers between devices with their start and end apart: 1, of which 1 were waited for; matrix products, arithmetic and copies ran while one was open for 0% of the time, Pallas kernels for 22%

profile of v4, /device:TPU:0, one launch (start us, length us, event | category | flops | bytes accessed | tf_op | source)
XLA Modules:
  0.0 92.4 jit_solution(8581679764787133178)
XLA Ops:
  0.6 6.0 %states.1 = (f32[64,72,128]{2,1,0:T(8,128)}, f32[160,512]{1,0:T(8,128)}, f32[8,2048]{1,0:T(8,128)}) custom-call(f32[32,512]{1,0:T(8,128)} %bitcast.3, f32[1,32]{1,0:T(1,128)} %bitcast.4, bf16[512,128]{1,0:T(8,128)(2,1)} %write_ref.5, bf16[512,128]{1,0:T(8,128)(2,1)} %read_ref.5, bf16[512,2048]{1,0:T(8,128)(2,1)} %act_ref.3, bf16[512,2048]{1,0:T(8,128)(2,1)} %up_ref.3), custom_call_target="tpu_custom_call" | custom-call | flops 536870912 | bytes 8388608 | tf_op jit(solution)/shard_map/states/pallas_call | solution.py:403
  6.7 11.5 %all-to-all-start = ((f32[64,72,128]{2,1,0:T(8,128)}), f32[64,72,128]{2,1,0:T(8,128)S(1)}, u32[]{:S(2)}, u32[]{:S(2)}) async-start(f32[64,72,128]{2,1,0:T(8,128)} %get-tuple-element.22), calls=%async_computation | async-start | bytes 4718592 | tf_op jit(solution)/shard_map/all_to_all | solution.py:430
  18.2 0.0 copy-start.4
  18.2 0.0 copy-start.5
  18.2 0.0 copy-start.6
  18.2 0.0 copy-start.7
  18.3 20.8 %local.1 = (bf16[512,2048]{1,0:T(8,128)(2,1)}, bf16[2048,512]{1,0:T(8,128)(2,1)}, bf16[2048,512]{1,0:T(8,128)(2,1)}, f32[2,144,2048]{2,1,0:T(8,128)}, f32[512,12...) custom-call(bf16[512,2048]{1,0:T(8,128)(2,1)} %act_ref.3, bf16[512,2048]{1,0:T(8,128)(2,1)} %up_ref.3, ...), custom_call_target="tpu_custom_call" | custom-call | flops 20000000000 | bytes 8388608 | tf_op jit(solution)/shard_map/local/pallas_call | solution.py:438
  39.0 12.6 %all-to-all-done.got_ref = f32[64,72,128]{2,1,0:T(8,128)S(1)} async-done(((f32[64,72,128]{2,1,0:T(8,128)}), f32[64,72,128]{2,1,0:T(8,128)S(1)}, u32[]{:S(2)}, u32[]{:S(2)}) %all-to-all-start) | async-done | bytes 2359328 | tf_op jit(solution)/shard_map/all_to_all | solution.py:430
  51.7 0.0 copy-start.8
  51.7 0.7 copy-done.8
  52.3 0.0 copy-start.1
  52.3 0.0 copy-start.2
  52.3 0.0 copy-start.3
  52.3 0.3 scan.1
  52.6 0.0 copy-start
  52.6 34.6 %all_to_all.10.carried_ref = f32[64,64,128]{2,1,0:T(8,128)S(1)} all-to-all(f32[64,64,128]{2,1,0:T(8,128)S(1)} %scan.1), channel_id=1, replica_groups=mesh['seq'=64,'dp'=2] {'seq'}, dimensions={0} | all-to-all | bytes 4194304 | tf_op jit(solution)/shard_map/all_to_all | solution.py:468
  87.2 0.0 copy-done.4
  87.2 0.0 copy-done.5
  87.2 0.0 copy-done.6
  87.2 0.0 copy-done.7
  87.2 0.0 copy-done.1
  87.2 0.0 copy-done.2
  87.2 0.0 copy-done.3
  87.2 0.0 copy-done
  87.2 5.2 %cross.1 = (bf16[512,2048]{1,0:T(8,128)(2,1)}, f32[32,512]{1,0:T(8,128)}, f32[512,128]{1,0:T(8,128)}, f32[512,128]{1,0:T(8,128)}) custom-call(bf16[2048,512]{1,0:T(8,128)(2,1)S(1)} %copy-done.2, bf16[2048,512]{1,0:T(8,128)(2,1)S(1)} %copy-done.3, bf16[512,2048]{1,0:T(8,128)(2,1)S(1)} %copy-done.1, ...), custom_call_target="tpu_custom_call", output_to_operand_aliasing={{2}: (9, {}), {3}: (10, {})} | custom-call | flops 1073741824 | bytes 16777216 | tf_op jit(solution)/shard_map/cross/pallas_call | solution.py:470
Async XLA Ops:
  6.7 45.0 %all-to-all-start = ((f32[64,72,128]{2,1,0:T(8,128)}), f32[64,72,128]{2,1,0:T(8,128)S(1)}, u32[]{:S(2)}, u32[]{:S(2)}) async-start(f32[64,72,128]{2,1,0:T(8,128)} %get-tuple-element.22), calls=%async_computation | async-start | bytes 4718592 | tf_op jit(solution)/shard_map/all_to_all | solution.py:430
  18.2 69.0 %copy-start.4 = (bf16[512,128]{1,0:T(8,128)(2,1)S(1)}, bf16[512,128]{1,0:T(8,128)(2,1)}, u32[]{:S(2)}) copy-start(bf16[512,128]{1,0:T(8,128)(2,1)} %write_ref.5) | copy-start | bytes 393220
  18.2 68.9 %copy-start.5 = (bf16[512,128]{1,0:T(8,128)(2,1)S(1)}, bf16[512,128]{1,0:T(8,128)(2,1)}, u32[]{:S(2)}) copy-start(bf16[512,128]{1,0:T(8,128)(2,1)} %read_ref.5) | copy-start | bytes 393220
  18.2 68.9 %copy-start.6 = (f32[160,512]{1,0:T(8,128)S(1)}, f32[160,512]{1,0:T(8,128)}, u32[]{:S(2)}) copy-start(f32[160,512]{1,0:T(8,128)} %get-tuple-element.18.running_ref.shifted_ref.out_ref.in_ref.tables_ref) | copy-start | bytes 983044
  18.2 68.9 %copy-start.7 = (f32[8,2048]{1,0:T(8,128)S(1)}, f32[8,2048]{1,0:T(8,128)}, u32[]{:S(2)}) copy-start(f32[8,2048]{1,0:T(8,128)} %get-tuple-element.25.spread_ref) | copy-start | bytes 196612
  51.7 0.7 copy-start.8
  52.3 34.9 %copy-start.1 = (bf16[512,2048]{1,0:T(8,128)(2,1)S(1)}, bf16[512,2048]{1,0:T(8,128)(2,1)}, u32[]{:S(2)}) copy-start(bf16[512,2048]{1,0:T(8,128)(2,1)} %get-tuple-element.21.back_ref) | copy-start | bytes 6291460
  52.3 34.9 %copy-start.2 = (bf16[2048,512]{1,0:T(8,128)(2,1)S(1)}, bf16[2048,512]{1,0:T(8,128)(2,1)}, u32[]{:S(2)}) copy-start(bf16[2048,512]{1,0:T(8,128)(2,1)} %get-tuple-element.19.act_scaled_ref) | copy-start | bytes 6291460
  52.3 34.9 %copy-start.3 = (bf16[2048,512]{1,0:T(8,128)(2,1)S(1)}, bf16[2048,512]{1,0:T(8,128)(2,1)}, u32[]{:S(2)}) copy-start(bf16[2048,512]{1,0:T(8,128)(2,1)} %get-tuple-element.20.up_scaled_ref) | copy-start | bytes 6291460
  52.6 34.6 %copy-start = (f32[2,144,2048]{2,1,0:T(8,128)S(1)}, f32[2,144,2048]{2,1,0:T(8,128)}, u32[]{:S(2)}) copy-start(f32[2,144,2048]{2,1,0:T(8,128)} %get-tuple-element.24.inside_ref) | copy-start | bytes 7077892

commit v5 on v4

--- a/solution.py
+++ b/solution.py
@@ -451,7 +451,7 @@
         ],
         out_shape=[low, low_across, low_across, jax.ShapeDtypeStruct((blocks, state + 2 * BUNCH, inner), F32), part, part, jax.ShapeDtypeStruct((8, LANES), F32)],
         scratch_shapes=[pltpu.VMEM((GROUP, GROUP), F32), pltpu.VMEM((GROUP, GROUP), F32)],
-        compiler_params=pltpu.CompilerParams(vmem_limit_bytes=56 * MIB),
+        compiler_params=pltpu.CompilerParams(vmem_limit_bytes=53 * MIB),
         cost_estimate=pl.CostEstimate(
             flops=20_000_000_000, bytes_accessed=8 * MIB, transcendentals=blocks * heads * GROUP * GROUP
         ),

time: 92.8 us -> 92.2 us (level)
  no operation moved by 1% of the time
where the time goes in v5:
time: 92.2 us; the launch traced here: 91.9 us
  blocking collectives  34.6 us (38%)
  Pallas kernels  31.7 us (34%)
  waiting for transfers between devices  13.3 us (14%)
  starting transfers between devices  11.6 us (13%)
    all_to_all x1, blocking collectives, on_device(): carried = lax.all_to_all(carried, 'seq', 0, 0)  34.6 us
    pallas_call x1, Pallas kernels, on_device(): pl.pallas_call(local_kernel, name='local', grid=(blocks, bunches), in_spe...  20.1 us
    all_to_all x1, waiting for transfers between devices, on_device(): got = lax.all_to_all(pieces, 'seq', 0, 0)  13.3 us
    all_to_all x1, starting transfers between devices, on_device(): got = lax.all_to_all(pieces, 'seq', 0, 0)  11.6 us
    pallas_call x1, Pallas kernels, on_device(): pl.pallas_call(partial(states_kernel, heads, piece_rows), name='states',...  6.05 us
    pallas_call x1, Pallas kernels, on_device(): pl.pallas_call(partial(cross_kernel, heads, piece_rows), name='cross', in...  5.22 us
  transfers between devices with their start and end apart: 1, of which 1 were waited for; matrix products, arithmetic and copies ran while one was open for 0% of the time, Pallas kernels for 22%

profile of v5, /device:TPU:0, one launch (start us, length us, event | category | flops | bytes accessed | tf_op | source)
XLA Modules:
  0.0 91.9 jit_solution(8312802980585399561)
XLA Ops:
  0.6 6.0 %states.1 = (f32[64,72,128]{2,1,0:T(8,128)}, f32[160,512]{1,0:T(8,128)}, f32[8,2048]{1,0:T(8,128)}) custom-call(f32[32,512]{1,0:T(8,128)} %bitcast.3, f32[1,32]{1,0:T(1,128)} %bitcast.4, bf16[512,128]{1,0:T(8,128)(2,1)} %write_ref.5, bf16[512,128]{1,0:T(8,128)(2,1)} %read_ref.5, bf16[512,2048]{1,0:T(8,128)(2,1)} %act_ref.3, bf16[512,2048]{1,0:T(8,128)(2,1)} %up_ref.3), custom_call_target="tpu_custom_call" | custom-call | flops 536870912 | bytes 8388608 | tf_op jit(solution)/shard_map/states/pallas_call | solution.py:403
  6.7 0.0 copy-start.4
  6.7 0.0 copy-start.5
  6.7 0.0 copy-start.6
  6.7 11.6 %all-to-all-start = ((f32[64,72,128]{2,1,0:T(8,128)}), f32[64,72,128]{2,1,0:T(8,128)S(1)}, u32[]{:S(2)}, u32[]{:S(2)}) async-start(f32[64,72,128]{2,1,0:T(8,128)} %get-tuple-element.22), calls=%async_computation | async-start | bytes 4718592 | tf_op jit(solution)/shard_map/all_to_all | solution.py:430
  18.4 0.0 copy-done.4
  18.4 0.0 copy-done.5
  18.4 0.0 copy-done.6
  18.4 0.0 copy-start.7
  18.4 20.1 %local.1 = (bf16[512,2048]{1,0:T(8,128)(2,1)}, bf16[2048,512]{1,0:T(8,128)(2,1)}, bf16[2048,512]{1,0:T(8,128)(2,1)}, f32[2,144,2048]{2,1,0:T(8,128)}, f32[512,12...) custom-call(bf16[512,2048]{1,0:T(8,128)(2,1)} %act_ref.3, bf16[512,2048]{1,0:T(8,128)(2,1)} %up_ref.3, ...), custom_call_target="tpu_custom_call" | custom-call | flops 20000000000 | bytes 8388608 | tf_op jit(solution)/shard_map/local/pallas_call | solution.py:438
  38.5 13.3 %all-to-all-done.got_ref = f32[64,72,128]{2,1,0:T(8,128)S(1)} async-done(((f32[64,72,128]{2,1,0:T(8,128)}), f32[64,72,128]{2,1,0:T(8,128)S(1)}, u32[]{:S(2)}, u32[]{:S(2)}) %all-to-all-start) | async-done | bytes 2359328 | tf_op jit(solution)/shard_map/all_to_all | solution.py:430
  51.8 0.0 copy-start.1
  51.8 0.0 copy-start.2
  51.8 0.0 copy-start.3
  51.8 0.3 scan.1
  52.1 0.0 copy-start
  52.1 34.6 %all_to_all.10.carried_ref = f32[64,64,128]{2,1,0:T(8,128)S(1)} all-to-all(f32[64,64,128]{2,1,0:T(8,128)S(1)} %scan.1), channel_id=1, replica_groups=mesh['seq'=64,'dp'=2] {'seq'}, dimensions={0} | all-to-all | bytes 4194304 | tf_op jit(solution)/shard_map/all_to_all | solution.py:468
  86.7 0.0 copy-done.7
  86.7 0.0 copy-done.1
  86.7 0.0 copy-done.2
  86.7 0.0 copy-done.3
  86.7 0.0 copy-done
  86.7 5.2 %cross.1 = (bf16[512,2048]{1,0:T(8,128)(2,1)}, f32[32,512]{1,0:T(8,128)}, f32[512,128]{1,0:T(8,128)}, f32[512,128]{1,0:T(8,128)}) custom-call(bf16[2048,512]{1,0:T(8,128)(2,1)S(1)} %copy-done.2, bf16[2048,512]{1,0:T(8,128)(2,1)S(1)} %copy-done.3, bf16[512,2048]{1,0:T(8,128)(2,1)S(1)} %copy-done.1, ...), custom_call_target="tpu_custom_call", output_to_operand_aliasing={{2}: (9, {}), {3}: (10, {})} | custom-call | flops 1073741824 | bytes 16777216 | tf_op jit(solution)/shard_map/cross/pallas_call | solution.py:470
Async XLA Ops:
  6.7 11.7 %copy-start.4 = (bf16[512,128]{1,0:T(8,128)(2,1)S(1)}, bf16[512,128]{1,0:T(8,128)(2,1)}, u32[]{:S(2)}) copy-start(bf16[512,128]{1,0:T(8,128)(2,1)} %write_ref.5) | copy-start | bytes 393220
  6.7 11.7 %copy-start.5 = (bf16[512,128]{1,0:T(8,128)(2,1)S(1)}, bf16[512,128]{1,0:T(8,128)(2,1)}, u32[]{:S(2)}) copy-start(bf16[512,128]{1,0:T(8,128)(2,1)} %read_ref.5) | copy-start | bytes 393220
  6.7 11.7 %copy-start.6 = (f32[160,512]{1,0:T(8,128)S(1)}, f32[160,512]{1,0:T(8,128)}, u32[]{:S(2)}) copy-start(f32[160,512]{1,0:T(8,128)} %get-tuple-element.18.running_ref.shifted_ref.out_ref.in_ref.tables_ref) | copy-start | bytes 983044
  6.7 45.1 %all-to-all-start = ((f32[64,72,128]{2,1,0:T(8,128)}), f32[64,72,128]{2,1,0:T(8,128)S(1)}, u32[]{:S(2)}, u32[]{:S(2)}) async-start(f32[64,72,128]{2,1,0:T(8,128)} %get-tuple-element.22), calls=%async_computation | async-start | bytes 4718592 | tf_op jit(solution)/shard_map/all_to_all | solution.py:430
  18.4 68.3 %copy-start.7 = (f32[8,2048]{1,0:T(8,128)S(1)}, f32[8,2048]{1,0:T(8,128)}, u32[]{:S(2)}) copy-start(f32[8,2048]{1,0:T(8,128)} %get-tuple-element.25.spread_ref) | copy-start | bytes 196612
  51.8 34.8 %copy-start.1 = (bf16[512,2048]{1,0:T(8,128)(2,1)S(1)}, bf16[512,2048]{1,0:T(8,128)(2,1)}, u32[]{:S(2)}) copy-start(bf16[512,2048]{1,0:T(8,128)(2,1)} %get-tuple-element.21.back_ref) | copy-start | bytes 6291460
  51.8 34.8 %copy-start.2 = (bf16[2048,512]{1,0:T(8,128)(2,1)S(1)}, bf16[2048,512]{1,0:T(8,128)(2,1)}, u32[]{:S(2)}) copy-start(bf16[2048,512]{1,0:T(8,128)(2,1)} %get-tuple-element.19.act_scaled_ref) | copy-start | bytes 6291460
  51.8 34.8 %copy-start.3 = (bf16[2048,512]{1,0:T(8,128)(2,1)S(1)}, bf16[2048,512]{1,0:T(8,128)(2,1)}, u32[]{:S(2)}) copy-start(bf16[2048,512]{1,0:T(8,128)(2,1)} %get-tuple-element.20.up_scaled_ref) | copy-start | bytes 6291460
  52.1 34.6 %copy-start = (f32[2,144,2048]{2,1,0:T(8,128)S(1)}, f32[2,144,2048]{2,1,0:T(8,128)}, u32[]{:S(2)}) copy-start(f32[2,144,2048]{2,1,0:T(8,128)} %get-tuple-element.24.inside_ref) | copy-start | bytes 7077892
